TPU v7x, 256 devices: a whole 4x4x8 slice. The times are simulated.
256 devices in a mesh: ctx: 32 (over y_hi, z, core), mp: 8 (over x, y_lo).
Axes of the slice: x: 4, y: 4 (y_hi: 2, y_lo: 2; y = y_hi * 2 + y_lo), z: 8, core: 2. Of those that a mesh axis runs over, the one named last changes fastest.
Arguments:
- query_heads: bfloat16 [4096, 8192], P('ctx', 'mp'), may hold values from -22 to 22
- key_heads: bfloat16 [4096, 1024], P('ctx', 'mp'), may hold values from -9 to 9
- value_heads: bfloat16 [4096, 1024], P('ctx', 'mp'), may hold values from -6 to 6
- residual_in: bfloat16 [4096, 8192], P('ctx', 'mp'), may hold values from -22 to 22
- norm_gain: bfloat16 [8192], P('mp'), may hold values from 0.5 to 2
- gate_weight: bfloat16 [8192, 14336], P('mp', 'ctx'), may hold values from -0.0625 to 0.0625
- up_weight: bfloat16 [8192, 14336], P('mp', 'ctx'), may hold values from -0.0625 to 0.0625
- doc_lengths: int32 [16], replicated, may hold values from 1 to 1024, 4096 in all
Outputs:
- residual: bfloat16 [4096, 8192], P('ctx', 'mp')
- hidden: bfloat16 [4096, 14336], P('mp', 'ctx')
Inputs may be any that keep to these rules, and one draw needn't show every extreme that they name: `doc_lengths`: the longest document has exactly 1024 tokens.
All inputs are finite; a program needn't handle non-finite values.
Results may differ from a plain program's by a relative error of at most 0.027.
Values may be sent and summed in bfloat16 or wider, within the bound.
A program may use at most 128 MiB of HBM per device.

v0:
```python
import jax
import jax.numpy as jnp
from jax import lax
from jax.sharding import PartitionSpec as P

D = 8192
HD = 128


def from_behind(block, axis, distance):
    devices = range(lax.axis_size(axis))
    route = [(i - distance, i) for i in devices if i - distance in devices]
    return lax.ppermute(block, axis, route)


def document_index(positions, doc_ends):
    return jnp.sum((positions[:, None] >= doc_ends[None, :]).astype(jnp.int32), axis=1)


def on_device(
    query_heads, key_heads, value_heads, residual_in, norm_gain, gate_weight, up_weight, doc_lengths
):
    local_rows = query_heads.shape[0]
    ctx_count = lax.axis_size("ctx")
    ctx_index = lax.axis_index("ctx")
    doc_ends = jnp.cumsum(doc_lengths)
    query_pos = ctx_index * local_rows + jnp.arange(local_rows, dtype=jnp.int32)
    query_doc = document_index(query_pos, doc_ends)
    kv_groups = key_heads.shape[1] // HD
    group_size = query_heads.shape[1] // HD // kv_groups
    query_split = query_heads.reshape(local_rows, kv_groups, group_size, HD)

    def attend(carried, key_piece, value_piece, offset):
        key_count = key_piece.shape[0]
        key_pos = offset + jnp.arange(key_count, dtype=jnp.int32)
        key_doc = document_index(key_pos, doc_ends)
        visible = (
            (query_doc[:, None] == key_doc[None, :])
            & (key_pos[None, :] <= query_pos[:, None])
            & (key_pos[None, :] >= 0)
        )

        def update(previous):
            running_max, denominator, weighted = previous
            key_split = key_piece.reshape(key_count, kv_groups, HD)
            value_split = value_piece.reshape(key_count, kv_groups, HD)
            scores = jnp.einsum(
                "qhgd,khd->hgqk", query_split, key_split, preferred_element_type=jnp.float32
            ) * HD ** (-0.5)
            scores = jnp.where(visible, scores, -1e30)
            new_max = jnp.maximum(running_max, jnp.max(scores, axis=-1))
            factor = jnp.exp(running_max - new_max)
            weights = jnp.where(visible, jnp.exp(scores - new_max[..., None]), 0.0)
            denominator = denominator * factor + jnp.sum(weights, axis=-1)
            weighted = weighted * factor[..., None] + jnp.einsum(
                "hgqk,khd->hgqd",
                weights.astype(jnp.bfloat16),
                value_split,
                preferred_element_type=jnp.float32,
            )
            return (new_max, denominator, weighted)

        return lax.cond(jnp.any(visible), update, lambda previous: previous, carried)

    starting = (
        jnp.full((kv_groups, group_size, local_rows), -1e30, jnp.float32),
        jnp.zeros((kv_groups, group_size, local_rows), jnp.float32),
        jnp.zeros((kv_groups, group_size, local_rows, HD), jnp.float32),
    )
    finished = attend(starting, key_heads, value_heads, ctx_index * local_rows)
    travelling = jnp.stack([key_heads, value_heads])
    for distance in range(1, ctx_count // 4 + 1):
        travelling = from_behind(travelling, "ctx", 1)
        finished = attend(
            finished, travelling[0], travelling[1], (ctx_index - distance) * local_rows
        )
    running_max, denominator, weighted = finished
    attended = jnp.transpose(weighted / denominator[..., None], (2, 0, 1, 3)).reshape(
        local_rows, kv_groups * group_size * HD
    )
    residual = (residual_in.astype(jnp.float32) + attended).astype(jnp.bfloat16)
    residual_float = residual.astype(jnp.float32)
    squares = lax.psum(jnp.sum(residual_float * residual_float, axis=1), "mp")
    inverse = lax.rsqrt(squares / D + 1e-05)
    normed = (residual_float * inverse[:, None] * norm_gain.astype(jnp.float32)[None, :]).astype(
        jnp.bfloat16
    )
    gathered = lax.all_gather(normed, "ctx", axis=0, tiled=True)
    hidden_width = gate_weight.shape[1]
    gate_part = jnp.dot(gathered, gate_weight, preferred_element_type=jnp.float32)
    up_part = jnp.dot(gathered, up_weight, preferred_element_type=jnp.float32)
    summed = lax.psum_scatter(
        jnp.concatenate([gate_part, up_part], axis=1).astype(jnp.bfloat16),
        "mp",
        scatter_dimension=0,
        tiled=True,
    ).astype(jnp.float32)
    gate_sum = summed[:, :hidden_width]
    up_sum = summed[:, hidden_width:]
    hidden = (jax.nn.silu(gate_sum) * up_sum).astype(jnp.bfloat16)
    return (residual, hidden)


def solution(mesh):
    in_specs = (
        P("ctx", "mp"),
        P("ctx", "mp"),
        P("ctx", "mp"),
        P("ctx", "mp"),
        P("mp"),
        P("mp", "ctx"),
        P("mp", "ctx"),
        P(),
    )
    out_specs = (P("ctx", "mp"), P("mp", "ctx"))
    return jax.shard_map(
        on_device, mesh=mesh, in_specs=in_specs, out_specs=out_specs, check_vma=False
    )
```

profile of v0, /device:TPU:25, one launch (start us, length us, event | category | flops | bytes accessed | tf_op | source)
XLA Modules:
  0.0 382.1 jit_solution(7357843601939263156)
XLA Ops:
  7.2 0.9 pad_maximum_fusion.1
  8.1 4.1 %collective-permute-start = (bf16[2,128,128]{2,1,0:T(8,128)(2,1)S(1)}, bf16[2,128,128]{2,1,0:T(8,128)(2,1)S(1)}, u32[]{:S(2)}, u32[]{:S(2)}) collective-permute-start(bf16[2,128,128]{2,1,0:T(8,128)(2,1)S(1)} %pad_maximum_fusion.1), channel_id=1, source_target_pairs={{0,8},{8,16},{16,24},{24,32},{32,40},{40,48},{48,56},{56,64},{64,7... | collective-permute-start | bytes 196616 | tf_op jit(solution)/shard_map/ppermute | solution.py:13
  13.3 1.1 and_and_fusion
  14.4 3.3 collective-permute-start.1
  17.8 0.9 fusion.153
  24.9 1.1 copy.52
  26.0 2.2 conditional.9
  26.0 1.0 fusion.157
  27.2 1.1 fusion
  28.3 2.5 collective-permute-start.2
  30.8 0.8 conditional.10
  31.7 2.0 collective-permute-done.2
  33.6 2.7 collective-permute-start.3
  37.2 5.6 %collective-permute-done.3 = bf16[2,128,128]{2,1,0:T(8,128)(2,1)S(1)} collective-permute-done((bf16[2,128,128]{2,1,0:T(8,128)(2,1)S(1)}, bf16[2,128,128]{2,1,0:T(8,128)(2,1)S(1)}, u32[]{:S(2)}, u32[]{:S(2)}) %collective-permute-start.3) | collective-permute-done | bytes 65568 | tf_op jit(solution)/shard_map/ppermute | solution.py:13
  42.8 1.9 collective-permute-start.4
  44.8 0.8 conditional.12
  45.6 6.4 %collective-permute-done.4 = bf16[2,128,128]{2,1,0:T(8,128)(2,1)S(1)} collective-permute-done((bf16[2,128,128]{2,1,0:T(8,128)(2,1)S(1)}, bf16[2,128,128]{2,1,0:T(8,128)(2,1)S(1)}, u32[]{:S(2)}, u32[]{:S(2)}) %collective-permute-start.4) | collective-permute-done | bytes 65568 | tf_op jit(solution)/shard_map/ppermute | solution.py:13
  52.0 1.9 collective-permute-start.5
  54.8 6.4 %collective-permute-done.5 = bf16[2,128,128]{2,1,0:T(8,128)(2,1)S(1)} collective-permute-done((bf16[2,128,128]{2,1,0:T(8,128)(2,1)S(1)}, bf16[2,128,128]{2,1,0:T(8,128)(2,1)S(1)}, u32[]{:S(2)}, u32[]{:S(2)}) %collective-permute-start.5) | collective-permute-done | bytes 65568 | tf_op jit(solution)/shard_map/ppermute | solution.py:13
  61.2 1.9 collective-permute-start.6
  64.0 6.6 %collective-permute-done.6 = bf16[2,128,128]{2,1,0:T(8,128)(2,1)} collective-permute-done((bf16[2,128,128]{2,1,0:T(8,128)(2,1)S(1)}, bf16[2,128,128]{2,1,0:T(8,128)(2,1)}, u32[]{:S(2)}, u32[]{:S(2)}) %collective-permute-start.6) | collective-permute-done | bytes 65568 | tf_op jit(solution)/shard_map/ppermute | solution.py:13
  70.6 1.9 collective-permute-start.7
  72.5 0.8 conditional.15
  73.4 6.6 %collective-permute-done.7 = bf16[2,128,128]{2,1,0:T(8,128)(2,1)S(1)} collective-permute-done((bf16[2,128,128]{2,1,0:T(8,128)(2,1)}, bf16[2,128,128]{2,1,0:T(8,128)(2,1)S(1)}, u32[]{:S(2)}, u32[]{:S(2)}) %collective-permute-start.7) | collective-permute-done | bytes 65568 | tf_op jit(solution)/shard_map/ppermute | solution.py:13
  80.7 12.6 %psum.7 = f32[128]{0:T(128)S(1)} all-reduce(f32[128]{0:T(128)S(1)} %get-tuple-element.421), channel_id=1, replica_groups=mesh['ctx'=32,'mp'=8] {'mp'}, use_global_device_ids=true, to_apply=%region_56.57 | all-reduce | flops 128 | bytes 1024 | tf_op jit(solution)/shard_map/psum | solution.py:83
  94.4 106.5 %all-gather.2.cloned.1.call-done = bf16[4096,1024]{1,0:T(8,128)(2,1)} async-done(((bf16[128,1024]{1,0:T(8,128)(2,1)}), bf16[4096,1024]{1,0:T(8,128)(2,1)}) %all-gather.2.cloned.1.call-update) | async-done | bytes 8388624 | tf_op jit(solution)/shard_map/all_gather | solution.py:88
  200.9 10.1 %convolution_convert_fusion = bf16[4096,448]{0,1:T(8,128)(2,1)} fusion(bf16[4096,1024]{1,0:T(8,128)(2,1)} %all-gather.2.cloned.1.call-done, bf16[1024,448]{0,1:T(8,128)(2,1)S(1)} %copy-done), kind=kOutput, calls=%fused_computation.186 | convolution fusion | flops 3759931392 | bytes 12976128 | tf_op jit(solution)/shard_map/dot_general | solution.py:91
  211.0 5.5 %convolution_convert_fusion.1 = bf16[4096,448]{0,1:T(8,128)(2,1)} fusion(bf16[4096,1024]{1,0:T(8,128)(2,1)S(1)} %copy-done.3, bf16[1024,448]{0,1:T(8,128)(2,1)S(1)} %copy-done.4), kind=kOutput, calls=%fused_computation.187 | convolution fusion | flops 3759931392 | bytes 12976128 | tf_op jit(solution)/shard_map/dot_general | solution.py:90
  216.5 7.1 %pad_maximum_fusion = bf16[4096,896]{0,1:T(8,128)(2,1)} fusion(bf16[4096,448]{0,1:T(8,128)(2,1)} %convolution_convert_fusion, bf16[4096,448]{0,1:T(8,128)(2,1)} %convolution_convert_fusion.1), kind=kLoop, calls=%fused_computation.185 | loop fusion | flops 14680064 | bytes 14680064 | tf_op jit(solution)/shard_map/concatenate | solution.py:93
  223.6 149.2 %reduce-scatter.2.cloned.1.call-done = bf16[512,896]{0,1:T(8,128)(2,1)} async-done(((bf16[4096,896]{0,1:T(8,128)(2,1)}), bf16[512,896]{0,1:T(8,128)(2,1)}) %reduce-scatter.2.cloned.1.call-update) | async-done | bytes 917520 | tf_op jit(solution)/shard_map/reduce_scatter | solution.py:92
  372.8 1.4 convert_element_type.127
  374.3 1.1 fusion.140
  (86 shorter events, 11.0 us)
Async XLA Ops:
  7.2 193.7 %copy-start = (bf16[1024,448]{0,1:T(8,128)(2,1)S(1)}, bf16[1024,448]{0,1:T(8,128)(2,1)}, u32[]{:S(2)}) copy-start(bf16[1024,448]{0,1:T(8,128)(2,1)} %param.32) | copy-start | bytes 2752516
  7.2 193.7 %all-gather.2.cloned.1.call-start = ((), (), s32[]{:S(2)}) async-start(), calls=%async_computation.1 | async-start | bytes 8650752 | tf_op jit(solution)/shard_map/all_gather | solution.py:88
  8.1 6.3 %collective-permute-start = (bf16[2,128,128]{2,1,0:T(8,128)(2,1)S(1)}, bf16[2,128,128]{2,1,0:T(8,128)(2,1)S(1)}, u32[]{:S(2)}, u32[]{:S(2)}) collective-permute-start(bf16[2,128,128]{2,1,0:T(8,128)(2,1)S(1)} %pad_maximum_fusion.1), channel_id=1, source_target_pairs={{0,8},{8,16},{16,24},{24,32},{32,40},{40,48},{48,56},{56,64},{64,7... | collective-permute-start | bytes 196616 | tf_op jit(solution)/shard_map/ppermute | solution.py:13
  14.4 13.8 %collective-permute-start.1 = (bf16[2,128,128]{2,1,0:T(8,128)(2,1)S(1)}, bf16[2,128,128]{2,1,0:T(8,128)(2,1)S(1)}, u32[]{:S(2)}, u32[]{:S(2)}) collective-permute-start(bf16[2,128,128]{2,1,0:T(8,128)(2,1)S(1)} %collective-permute-done), channel_id=1, source_target_pairs={{0,8},{8,16},{16,24},{24,32},{32,40},{40,48},{48,56},{56,64},{64,7... | collective-permute-start | bytes 196616 | tf_op jit(solution)/shard_map/ppermute | solution.py:13
  28.3 5.4 %collective-permute-start.2 = (bf16[2,128,128]{2,1,0:T(8,128)(2,1)S(1)}, bf16[2,128,128]{2,1,0:T(8,128)(2,1)S(1)}, u32[]{:S(2)}, u32[]{:S(2)}) collective-permute-start(bf16[2,128,128]{2,1,0:T(8,128)(2,1)S(1)} %collective-permute-done.1), channel_id=1, source_target_pairs={{0,8},{8,16},{16,24},{24,32},{32,40},{40,48},{48,56},{56,64},{64,7... | collective-permute-start | bytes 196616 | tf_op jit(solution)/shard_map/ppermute | solution.py:13
  33.6 9.2 %collective-permute-start.3 = (bf16[2,128,128]{2,1,0:T(8,128)(2,1)S(1)}, bf16[2,128,128]{2,1,0:T(8,128)(2,1)S(1)}, u32[]{:S(2)}, u32[]{:S(2)}) collective-permute-start(bf16[2,128,128]{2,1,0:T(8,128)(2,1)S(1)} %collective-permute-done.2), channel_id=1, source_target_pairs={{0,8},{8,16},{16,24},{24,32},{32,40},{40,48},{48,56},{56,64},{64,7... | collective-permute-start | bytes 196616 | tf_op jit(solution)/shard_map/ppermute | solution.py:13
  42.8 9.2 %collective-permute-start.4 = (bf16[2,128,128]{2,1,0:T(8,128)(2,1)S(1)}, bf16[2,128,128]{2,1,0:T(8,128)(2,1)S(1)}, u32[]{:S(2)}, u32[]{:S(2)}) collective-permute-start(bf16[2,128,128]{2,1,0:T(8,128)(2,1)S(1)} %collective-permute-done.3), channel_id=1, source_target_pairs={{0,8},{8,16},{16,24},{24,32},{32,40},{40,48},{48,56},{56,64},{64,7... | collective-permute-start | bytes 196616 | tf_op jit(solution)/shard_map/ppermute | solution.py:13
  52.0 9.2 %collective-permute-start.5 = (bf16[2,128,128]{2,1,0:T(8,128)(2,1)S(1)}, bf16[2,128,128]{2,1,0:T(8,128)(2,1)S(1)}, u32[]{:S(2)}, u32[]{:S(2)}) collective-permute-start(bf16[2,128,128]{2,1,0:T(8,128)(2,1)S(1)} %collective-permute-done.4), channel_id=1, source_target_pairs={{0,8},{8,16},{16,24},{24,32},{32,40},{40,48},{48,56},{56,64},{64,7... | collective-permute-start | bytes 196616 | tf_op jit(solution)/shard_map/ppermute | solution.py:13
  61.2 9.4 %collective-permute-start.6 = (bf16[2,128,128]{2,1,0:T(8,128)(2,1)S(1)}, bf16[2,128,128]{2,1,0:T(8,128)(2,1)}, u32[]{:S(2)}, u32[]{:S(2)}) collective-permute-start(bf16[2,128,128]{2,1,0:T(8,128)(2,1)S(1)} %collective-permute-done.5), channel_id=1, source_target_pairs={{0,8},{8,16},{16,24},{24,32},{32,40},{40,48},{48,56},{56,64},{64,7... | collective-permute-start | bytes 196616 | tf_op jit(solution)/shard_map/ppermute | solution.py:13
  63.1 17.3 %copy-start.2 = (bf16[128,1024]{1,0:T(8,128)(2,1)S(1)}, bf16[128,1024]{1,0:T(8,128)(2,1)}, u32[]{:S(2)}) copy-start(bf16[128,1024]{1,0:T(8,128)(2,1)} %param.29) | copy-start | bytes 786436
  70.6 9.4 %collective-permute-start.7 = (bf16[2,128,128]{2,1,0:T(8,128)(2,1)}, bf16[2,128,128]{2,1,0:T(8,128)(2,1)S(1)}, u32[]{:S(2)}, u32[]{:S(2)}) collective-permute-start(bf16[2,128,128]{2,1,0:T(8,128)(2,1)} %collective-permute-done.6), channel_id=1, source_target_pairs={{0,8},{8,16},{16,24},{24,32},{32,40},{40,48},{48,56},{56,64},{64,7... | collective-permute-start | bytes 196616 | tf_op jit(solution)/shard_map/ppermute | solution.py:13
  80.7 130.3 %copy-start.1 = (bf16[128,1024]{1,0:T(8,128)(2,1)}, bf16[128,1024]{1,0:T(8,128)(2,1)S(1)}, u32[]{:S(2)}) copy-start(bf16[128,1024]{1,0:T(8,128)(2,1)S(1)} %get-tuple-element.422) | copy-start | bytes 786436
  94.1 116.8 %copy-start.4 = (bf16[1024,448]{0,1:T(8,128)(2,1)S(1)}, bf16[1024,448]{0,1:T(8,128)(2,1)}, u32[]{:S(2)}) copy-start(bf16[1024,448]{0,1:T(8,128)(2,1)} %param.31) | copy-start | bytes 2752516
  94.2 278.7 %reduce-scatter.2.cloned.1.call-start = ((), (), s32[]{:S(2)}) async-start(), calls=%async_computation.2 | async-start | bytes 8257536 | tf_op jit(solution)/shard_map/reduce_scatter | solution.py:92
  200.9 10.1 %copy-start.3 = (bf16[4096,1024]{1,0:T(8,128)(2,1)S(1)}, bf16[4096,1024]{1,0:T(8,128)(2,1)}, u32[]{:S(2)}) copy-start(bf16[4096,1024]{1,0:T(8,128)(2,1)} %all-gather.2.cloned.1.call-done) | copy-start | bytes 25165828
Sparse Core Ops, SparseCore 0:
  94.3 106.5 all-gather.1
  223.7 149.0 reduce-scatter.1
where the time goes:
time: 385 us; the launch traced here: 382 us
  waiting for transfers between devices  289 us (75%)
  matrix products  21.6 us (6%)
  starting transfers between devices  20.6 us (5%)
  between operations  19.9 us (5%)
  other arithmetic  15.5 us (4%)
  blocking collectives  12.6 us (3%)
    reduce_scatter x1, waiting for transfers between devices, on_device(): lax.psum_scatter(jnp.concatenate([gate_part, up_part], axis=1).astype(jnp...  149 us
    all_gather x1, waiting for transfers between devices, on_device(): gathered = lax.all_gather(normed, 'ctx', axis=0, tiled=True)  107 us
    ppermute x8, waiting for transfers between devices, from_behind(): return lax.ppermute(block, axis, route)  33.5 us
    ppermute x8, starting transfers between devices, from_behind(): return lax.ppermute(block, axis, route)  20.3 us
    psum x1, blocking collectives, on_device(): squares = lax.psum(jnp.sum(residual_float * residual_float, axis=1), 'mp')  12.6 us
    dot_general x1, matrix products, on_device(): up_part = jnp.dot(gathered, up_weight, preferred_element_type=jnp.float32)  10.1 us
  transfers between devices with their start and end apart: 10, of which 8 were waited for; matrix products, arithmetic and copies ran while one was open for 3% of the time, Pallas kernels for 0%

commit v1 on v0

--- a/solution.py
+++ b/solution.py
@@ -1,10 +1,312 @@
+import functools
+
 import jax
 import jax.numpy as jnp
 from jax import lax
+from jax.experimental import pallas as pl
+from jax.experimental.pallas import tpu as pltpu
 from jax.sharding import PartitionSpec as P
 
 D = 8192
 HD = 128
+MESH = pl.DeviceIdType.MESH
+ROWS = 128
+KB = 1024
+WIDTH_A = 512
+WIDTH_B = 384
+PARTS = ((0, WIDTH_A), (WIDTH_A, WIDTH_B))
+WIDTH = WIDTH_A + WIDTH_B
+
+
+def place():
+    ctx = lax.axis_index("ctx")
+    mp = lax.axis_index("mp")
+    return ctx // 16, lax.rem(ctx // 2, 8), lax.rem(ctx, 2), mp // 2, lax.rem(mp, 2)
+
+
+def device(yh, z, c, x, yl):
+    return (yh * 16 + z * 2 + c, x * 2 + yl)
+
+
+def pick(w, values):
+    out = jnp.int32(values[0])
+    for i in range(1, len(values)):
+        out = jnp.where(w == i, jnp.int32(values[i]), out)
+    return out
+
+
+OFFSETS = ((0, 0, -1, 1), (1, -1, 2, -2), (-3, 3, -2, 2), (4, -4, 3, -3))
+ONWARD_UP = ((1, 1, 1, 0), (0, 1, 0, 1), (1, 0, 1, 0), (0, 0, 0, 0))
+ONWARD_DOWN = ((1, 1, 0, 1), (1, 0, 1, 0), (0, 1, 0, 1), (0, 0, 0, 0))
+ORDER = ((0, 0), (1, 0), (2, 0), (0, 1), (3, 0), (1, 1), (2, 1), (3, 1))
+FIRST = 4
+
+
+def ffn_kernel(
+    normed_ref, gate_ref, up_ref, out_ref,
+    tokens, weights, staged, landed, own_sum,
+    w_send, w_recv, cross_send, tok_recv, up_send, down_send, sib_send, hi_send, sum_send, sum_recv,
+):
+    yh, z, c, x, yl = place()
+    match = lax.rem(z // 2, 2) == yl
+    w = lax.rem(z - 2 * yl + 8, 4)
+    my_source = (z // 4) * 2 + lax.rem(z, 2)
+    sibling = device(yh, z, 1 - c, x, yl)
+    lo_partner = device(yh, z, c, x, 1 - yl)
+    hi_partner = device(1 - yh, z, c, x, yl)
+    above = device(yh, lax.rem(z + 1, 8), c, x, yl)
+    below = device(yh, lax.rem(z + 7, 8), c, x, yl)
+    x_peers = [device(yh, z, c, lax.rem(x + d, 4), yl) for d in (1, 2, 3)]
+    mine = pl.ds(pl.multiple_of(c * ROWS, ROWS), ROWS)
+
+    barrier = pltpu.get_barrier_semaphore()
+    peers = [sibling, lo_partner, hi_partner, above, below] + x_peers
+    for peer in peers:
+        pl.semaphore_signal(barrier, inc=1, device_id=peer, device_id_type=MESH)
+
+    weights[yl, :, 0:256] = gate_ref[:, 0:256]
+    weights[yl, :, 256:512] = up_ref[:, 0:256]
+    weights[yl, :, 512:640] = gate_ref[:, 256:384]
+    weights[yl, :, 640:768] = up_ref[:, 256:384]
+    weights[yl, :, 768:896] = jnp.concatenate([gate_ref[:, 384:448], up_ref[:, 384:448]], axis=1)
+    pl.semaphore_wait(barrier, len(peers))
+
+    def weight_copy(part):
+        start, size = PARTS[part]
+        view = weights.at[yl, :, pl.ds(start, size)]
+        return pltpu.make_async_remote_copy(
+            src_ref=view, dst_ref=view, send_sem=w_send.at[part], recv_sem=w_recv.at[part],
+            device_id=lo_partner, device_id_type=MESH,
+        )
+
+    def cross_copy():
+        return pltpu.make_async_remote_copy(
+            src_ref=normed_ref, dst_ref=tokens.at[yh, my_source, yl, mine],
+            send_sem=cross_send.at[0], recv_sem=tok_recv.at[yh, my_source, yl, c],
+            device_id=lo_partner, device_id_type=MESH,
+        )
+
+    def token_copy(h, source, kb, sems, target):
+        view = tokens.at[h, source, kb, mine]
+        return pltpu.make_async_remote_copy(
+            src_ref=view, dst_ref=view, send_sem=sems.at[h, source, kb],
+            recv_sem=tok_recv.at[h, source, kb, c], device_id=target, device_id_type=MESH,
+        )
+
+    def token_arrival(h, source, kb, core):
+        view = tokens.at[h, source, kb, pl.ds(pl.multiple_of(core * ROWS, ROWS), ROWS)]
+        return pltpu.make_async_remote_copy(
+            src_ref=view, dst_ref=view, send_sem=sib_send.at[h, source, kb],
+            recv_sem=tok_recv.at[h, source, kb, core], device_id=sibling, device_id_type=MESH,
+        )
+
+    def unit_of(step):
+        unit = pick(step, [u for u, _ in ORDER])
+        half = pick(step, [h for _, h in ORDER])
+        table = lambda rows: pick(unit * 4 + w, [v for row in rows for v in row])
+        source_z = lax.rem(z + table(OFFSETS) + 8, 8)
+        source = (source_z // 4) * 2 + lax.rem(source_z, 2)
+        h = lax.rem(yh + half, 2)
+        own = jnp.logical_and(match, unit == 0)
+        return h, half, source, own, table(ONWARD_UP) == 1, table(ONWARD_DOWN) == 1
+
+    def order_of_blocks(i):
+        return lax.rem(yl + i, 2)
+
+    def handle(step):
+        h, half, source, own, go_up, go_down = unit_of(step)
+        at_home = jnp.logical_and(own, half == 0)
+        for i in range(2):
+            kb = order_of_blocks(i)
+            if i == 0:
+                @pl.when(jnp.logical_not(at_home))
+                def _():
+                    token_arrival(h, source, kb, c).wait_recv()
+            else:
+                token_arrival(h, source, kb, c).wait_recv()
+
+            @pl.when(go_up)
+            def _():
+                token_copy(h, source, kb, up_send, above).start()
+
+            @pl.when(go_down)
+            def _():
+                token_copy(h, source, kb, down_send, below).start()
+
+            token_copy(h, source, kb, sib_send, sibling).start()
+
+            @pl.when(at_home)
+            def _():
+                token_copy(h, source, kb, hi_send, hi_partner).start()
+
+    def sum_copy(h, source, part, peer):
+        start, size = PARTS[part]
+        low = lax.rem(source, 2)
+        owner = h * 2 + source // 2
+        slot = lax.rem(x - owner + 4, 4) - 1
+        return pltpu.make_async_remote_copy(
+            src_ref=staged.at[h, source, :, pl.ds(start, size)],
+            dst_ref=landed.at[slot, low, :, pl.ds(start, size)],
+            send_sem=sum_send.at[h, source, part], recv_sem=sum_recv.at[slot, low, part],
+            device_id=device(yh, z, c, owner, yl), device_id_type=MESH,
+        )
+
+    def multiply(step, part):
+        h, _, source, _, _, _ = unit_of(step)
+        start, size = PARTS[part]
+        columns = pl.ds(start, size)
+        product = jnp.dot(
+            tokens[h, source, 0], weights[0, :, columns], preferred_element_type=jnp.float32
+        ) + jnp.dot(
+            tokens[h, source, 1], weights[1, :, columns], preferred_element_type=jnp.float32
+        )
+        owned = h * 2 + source // 2 == x
+
+        @pl.when(owned)
+        def _():
+            own_sum[lax.rem(source, 2), :, columns] = product
+
+        @pl.when(jnp.logical_not(owned))
+        def _():
+            staged[h, source, :, columns] = product.astype(jnp.bfloat16)
+            sum_copy(h, source, part, None).start()
+
+    def sibling_arrived(step):
+        h, _, source, _, _, _ = unit_of(step)
+        for i in range(2):
+            token_arrival(h, source, i, 1 - c).wait_recv()
+
+    @pl.when(match)
+    def _():
+        tokens[yh, my_source, yl, mine] = normed_ref[...]
+
+    @pl.when(jnp.logical_not(match))
+    def _():
+        cross_copy().start()
+
+    for part in range(2):
+        weight_copy(part).start()
+
+    def weights_arrived(part):
+        start, size = PARTS[part]
+        view = weights.at[1 - yl, :, pl.ds(start, size)]
+        pltpu.make_async_remote_copy(
+            src_ref=view, dst_ref=view, send_sem=w_send.at[part], recv_sem=w_recv.at[part],
+            device_id=lo_partner, device_id_type=MESH,
+        ).wait_recv()
+
+    handle(0)
+    weights_arrived(0)
+
+    def first(step, _):
+        handle(step + 1)
+        sibling_arrived(step)
+        multiply(step, 0)
+        return 0
+
+    lax.fori_loop(0, FIRST, first, 0)
+    weights_arrived(1)
+
+    def catch_up(step, _):
+        multiply(step, 1)
+        return 0
+
+    lax.fori_loop(0, FIRST, catch_up, 0)
+
+    def second(step, _):
+        @pl.when(step < 7)
+        def _():
+            handle(step + 1)
+
+        sibling_arrived(step)
+        multiply(step, 0)
+        multiply(step, 1)
+        return 0
+
+    lax.fori_loop(FIRST, 8, second, 0)
+
+    def finish(low, _):
+        rows = pl.ds(pl.multiple_of(low * 256, 256), 256)
+        totals = []
+        for part in range(2):
+            start, size = PARTS[part]
+            columns = pl.ds(start, size)
+            total = own_sum[low, :, columns]
+            for slot in range(3):
+                view = landed.at[slot, low, :, columns]
+                pltpu.make_async_remote_copy(
+                    src_ref=view, dst_ref=view, send_sem=sum_send.at[0, 0, part],
+                    recv_sem=sum_recv.at[slot, low, part], device_id=x_peers[0], device_id_type=MESH,
+                ).wait_recv()
+                total = total + landed[slot, low, :, columns].astype(jnp.float32)
+            totals.append(total)
+        a, b = totals
+        silu = lambda v: v / (1.0 + jnp.exp(-v))
+        out_ref[rows, 0:256] = (silu(a[:, :256]) * a[:, 256:]).astype(jnp.bfloat16)
+        out_ref[rows, 256:384] = (silu(b[:, :128]) * b[:, 128:256]).astype(jnp.bfloat16)
+        tail = b[:, 256:384]
+        mixed = silu(tail) * pltpu.roll(tail, 64, 1)
+        out_ref[rows, 384:448] = mixed[:, :64].astype(jnp.bfloat16)
+        return 0
+
+    lax.fori_loop(0, 2, finish, 0)
+
+    for part in range(2):
+        weight_copy(part).wait_send()
+
+    @pl.when(jnp.logical_not(match))
+    def _():
+        cross_copy().wait_send()
+
+    def drain(step, _):
+        h, half, source, own, go_up, go_down = unit_of(step)
+        for kb in range(2):
+            @pl.when(go_up)
+            def _():
+                token_copy(h, source, kb, up_send, above).wait_send()
+
+            @pl.when(go_down)
+            def _():
+                token_copy(h, source, kb, down_send, below).wait_send()
+
+            token_copy(h, source, kb, sib_send, sibling).wait_send()
+
+            @pl.when(jnp.logical_and(own, half == 0))
+            def _():
+                token_copy(h, source, kb, hi_send, hi_partner).wait_send()
+
+        @pl.when(h * 2 + source // 2 != x)
+        def _():
+            for part in range(2):
+                sum_copy(h, source, part, None).wait_send()
+        return 0
+
+    lax.fori_loop(0, 8, drain, 0)
+
+
+def feed_forward(normed, gate_weight, up_weight):
+    dma = pltpu.SemaphoreType.DMA
+    vmem = pl.BlockSpec(memory_space=pltpu.VMEM)
+    return pl.pallas_call(
+        ffn_kernel,
+        out_shape=jax.ShapeDtypeStruct((512, 448), jnp.bfloat16),
+        in_specs=[vmem] * 3,
+        out_specs=vmem,
+        scratch_shapes=[
+            pltpu.VMEM((2, 4, 2, 2 * ROWS, KB), jnp.bfloat16),
+            pltpu.VMEM((2, KB, WIDTH), jnp.bfloat16),
+            pltpu.VMEM((2, 4, 2 * ROWS, WIDTH), jnp.bfloat16),
+            pltpu.VMEM((3, 2, 2 * ROWS, WIDTH), jnp.bfloat16),
+            pltpu.VMEM((2, 2 * ROWS, WIDTH), jnp.float32),
+            dma((2,)), dma((2,)), dma((1,)), dma((2, 4, 2, 2)),
+            dma((2, 4, 2)), dma((2, 4, 2)), dma((2, 4, 2)), dma((2, 4, 2)),
+            dma((2, 4, 2)), dma((3, 2, 2)),
+        ],
+        compiler_params=pltpu.CompilerParams(
+            collective_id=0, has_side_effects=True, vmem_limit_bytes=56 * 2**20
+        ),
+        name="feed_forward",
+    )(normed, gate_weight, up_weight)
 
 
 def from_behind(block, axis, distance):
@@ -85,19 +387,7 @@
     normed = (residual_float * inverse[:, None] * norm_gain.astype(jnp.float32)[None, :]).astype(
         jnp.bfloat16
     )
-    gathered = lax.all_gather(normed, "ctx", axis=0, tiled=True)
-    hidden_width = gate_weight.shape[1]
-    gate_part = jnp.dot(gathered, gate_weight, preferred_element_type=jnp.float32)
-    up_part = jnp.dot(gathered, up_weight, preferred_element_type=jnp.float32)
-    summed = lax.psum_scatter(
-        jnp.concatenate([gate_part, up_part], axis=1).astype(jnp.bfloat16),
-        "mp",
-        scatter_dimension=0,
-        tiled=True,
-    ).astype(jnp.float32)
-    gate_sum = summed[:, :hidden_width]
-    up_sum = summed[:, hidden_width:]
-    hidden = (jax.nn.silu(gate_sum) * up_sum).astype(jnp.bfloat16)
+    hidden = feed_forward(normed, gate_weight, up_weight)
     return (residual, hidden)
 
 

time: 385 us -> 238 us (0.62)
  the two profiles are of different devices: /device:TPU:25 before, /device:TPU:39 now
where the time goes in v1:
time: 238 us
  Pallas kernels  166 us (70%)
  starting transfers between devices  31.3 us (13%)
  blocking collectives  12.6 us (5%)
  local copies, waits for them, and re-layouts  7.51 us (3%)
  between operations  6.55 us (3%)
  waiting for transfers between devices  6.29 us (3%)
  other arithmetic  5.51 us (2%)
    pallas_call x1, Pallas kernels, feed_forward(): pl.pallas_call(ffn_kernel, out_shape=jax.ShapeDtypeStruct((512, 448), jnp...  166 us
    ppermute x8, starting transfers between devices, from_behind(): return lax.ppermute(block, axis, route)  31.3 us
    psum x1, blocking collectives, on_device(): squares = lax.psum(jnp.sum(residual_float * residual_float, axis=1), 'mp')  12.6 us
    unnamed x16, local copies, waits for them, and re-layouts  6.42 us
    ppermute x8, waiting for transfers between devices, from_behind(): return lax.ppermute(block, axis, route)  6.29 us
  transfers between devices with their start and end apart: 8, of which 6 were waited for; matrix products, arithmetic and copies ran while one was open for 4% of the time, Pallas kernels for 0%

profile of v1, /device:TPU:39, one launch (start us, length us, event | category | flops | bytes accessed | tf_op | source)
XLA Modules:
  0.0 237.7 jit_solution(13652101615781237035)
XLA Ops:
  0.6 0.9 pad_maximum_fusion
  1.5 4.1 %collective-permute-start = (bf16[2,128,128]{2,1,0:T(8,128)(2,1)S(1)}, bf16[2,128,128]{2,1,0:T(8,128)(2,1)S(1)}, u32[]{:S(2)}, u32[]{:S(2)}) collective-permute-start(bf16[2,128,128]{2,1,0:T(8,128)(2,1)S(1)} %pad_maximum_fusion), channel_id=1, source_target_pairs={{0,8},{8,16},{16,24},{24,32},{32,40},{40,48},{48,56},{56,64},{64,7... | collective-permute-start | bytes 196616 | tf_op jit(solution)/shard_map/ppermute | solution.py:315
  5.7 0.7 copy.57
  6.7 1.1 and_and_fusion
  7.8 3.3 %collective-permute-start.1 = (bf16[2,128,128]{2,1,0:T(8,128)(2,1)S(1)}, bf16[2,128,128]{2,1,0:T(8,128)(2,1)S(1)}, u32[]{:S(2)}, u32[]{:S(2)}) collective-permute-start(bf16[2,128,128]{2,1,0:T(8,128)(2,1)S(1)} %collective-permute-done), channel_id=1, source_target_pairs={{0,8},{8,16},{16,24},{24,32},{32,40},{40,48},{48,56},{56,64},{64,7... | collective-permute-start | bytes 196616 | tf_op jit(solution)/shard_map/ppermute | solution.py:315
  11.2 1.0 fusion.152
  12.1 0.7 convert_element_type.118
  18.4 1.1 copy.58
  19.5 1.3 copy.69.gate_ref
  20.9 1.3 copy.70.up_ref
  22.2 0.7 conditional.9
  22.9 2.5 %collective-permute-start.2 = (bf16[2,128,128]{2,1,0:T(8,128)(2,1)S(1)}, bf16[2,128,128]{2,1,0:T(8,128)(2,1)S(1)}, u32[]{:S(2)}, u32[]{:S(2)}) collective-permute-start(bf16[2,128,128]{2,1,0:T(8,128)(2,1)S(1)} %collective-permute-done.1), channel_id=1, source_target_pairs={{0,8},{8,16},{16,24},{24,32},{32,40},{40,48},{48,56},{56,64},{64,7... | collective-permute-start | bytes 196616 | tf_op jit(solution)/shard_map/ppermute | solution.py:315
  25.4 0.8 conditional.10
  25.7 0.4 fusion.16
  26.3 0.4 collective-permute-done.2
  26.7 4.3 %collective-permute-start.3 = (bf16[2,128,128]{2,1,0:T(8,128)(2,1)S(1)}, bf16[2,128,128]{2,1,0:T(8,128)(2,1)S(1)}, u32[]{:S(2)}, u32[]{:S(2)}) collective-permute-start(bf16[2,128,128]{2,1,0:T(8,128)(2,1)S(1)} %collective-permute-done.2), channel_id=1, source_target_pairs={{0,8},{8,16},{16,24},{24,32},{32,40},{40,48},{48,56},{56,64},{64,7... | collective-permute-start | bytes 196616 | tf_op jit(solution)/shard_map/ppermute | solution.py:315
  31.0 0.8 conditional.11
  31.3 0.4 fusion.31
  31.9 0.4 collective-permute-done.3
  32.3 4.3 %collective-permute-start.4 = (bf16[2,128,128]{2,1,0:T(8,128)(2,1)S(1)}, bf16[2,128,128]{2,1,0:T(8,128)(2,1)S(1)}, u32[]{:S(2)}, u32[]{:S(2)}) collective-permute-start(bf16[2,128,128]{2,1,0:T(8,128)(2,1)S(1)} %collective-permute-done.3), channel_id=1, source_target_pairs={{0,8},{8,16},{16,24},{24,32},{32,40},{40,48},{48,56},{56,64},{64,7... | collective-permute-start | bytes 196616 | tf_op jit(solution)/shard_map/ppermute | solution.py:315
  36.6 1.3 collective-permute-done.4
  37.9 4.3 %collective-permute-start.5 = (bf16[2,128,128]{2,1,0:T(8,128)(2,1)S(1)}, bf16[2,128,128]{2,1,0:T(8,128)(2,1)S(1)}, u32[]{:S(2)}, u32[]{:S(2)}) collective-permute-start(bf16[2,128,128]{2,1,0:T(8,128)(2,1)S(1)} %collective-permute-done.4), channel_id=1, source_target_pairs={{0,8},{8,16},{16,24},{24,32},{32,40},{40,48},{48,56},{56,64},{64,7... | collective-permute-start | bytes 196616 | tf_op jit(solution)/shard_map/ppermute | solution.py:315
  42.2 1.3 collective-permute-done.5
  43.5 4.3 %collective-permute-start.6 = (bf16[2,128,128]{2,1,0:T(8,128)(2,1)S(1)}, bf16[2,128,128]{2,1,0:T(8,128)(2,1)}, u32[]{:S(2)}, u32[]{:S(2)}) collective-permute-start(bf16[2,128,128]{2,1,0:T(8,128)(2,1)S(1)} %collective-permute-done.5), channel_id=1, source_target_pairs={{0,8},{8,16},{16,24},{24,32},{32,40},{40,48},{48,56},{56,64},{64,7... | collective-permute-start | bytes 196616 | tf_op jit(solution)/shard_map/ppermute | solution.py:315
  47.8 1.3 collective-permute-done.6
  49.0 4.4 %collective-permute-start.7 = (bf16[2,128,128]{2,1,0:T(8,128)(2,1)}, bf16[2,128,128]{2,1,0:T(8,128)(2,1)S(1)}, u32[]{:S(2)}, u32[]{:S(2)}) collective-permute-start(bf16[2,128,128]{2,1,0:T(8,128)(2,1)} %collective-permute-done.6), channel_id=1, source_target_pairs={{0,8},{8,16},{16,24},{24,32},{32,40},{40,48},{48,56},{56,64},{64,7... | collective-permute-start | bytes 196616 | tf_op jit(solution)/shard_map/ppermute | solution.py:315
  53.5 1.6 collective-permute-done.7
  55.6 0.6 copy-done.3
  56.4 12.6 %psum.7 = f32[128]{0:T(128)S(1)} all-reduce(f32[128]{0:T(128)S(1)} %get-tuple-element.427), channel_id=1, replica_groups=mesh['ctx'=32,'mp'=8] {'mp'}, use_global_device_ids=true, to_apply=%region_56.57 | all-reduce | flops 128 | bytes 1024 | tf_op jit(solution)/shard_map/psum | solution.py:385
  69.0 0.8 fusion.142.normed_ref
  69.8 165.9 %feed_forward.1 = bf16[512,448]{1,0:T(8,128)(2,1)} custom-call(bf16[128,1024]{1,0:T(8,128)(2,1)} %fusion.142.normed_ref, bf16[1024,448]{1,0:T(8,128)(2,1)} %copy.69.gate_ref, bf16[1024,448]{1,0:T(8,128)(2,1)} %copy.70.up_ref), custom_call_target="tpu_custom_call" | custom-call | tf_op jit(solution)/shard_map/feed_forward/pallas_call | solution.py:290
  235.7 2.0 copy.71
  (57 shorter events, 2.5 us)
Async XLA Ops:
  0.6 18.9 %copy-start.1 = (bf16[1024,448]{0,1:T(8,128)(2,1)S(1)}, bf16[1024,448]{0,1:T(8,128)(2,1)}, u32[]{:S(2)}) copy-start(bf16[1024,448]{0,1:T(8,128)(2,1)} %param.31) | copy-start | bytes 2752516
  1.5 6.3 %collective-permute-start = (bf16[2,128,128]{2,1,0:T(8,128)(2,1)S(1)}, bf16[2,128,128]{2,1,0:T(8,128)(2,1)S(1)}, u32[]{:S(2)}, u32[]{:S(2)}) collective-permute-start(bf16[2,128,128]{2,1,0:T(8,128)(2,1)S(1)} %pad_maximum_fusion), channel_id=1, source_target_pairs={{0,8},{8,16},{16,24},{24,32},{32,40},{40,48},{48,56},{56,64},{64,7... | collective-permute-start | bytes 196616 | tf_op jit(solution)/shard_map/ppermute | solution.py:315
  7.8 15.1 %collective-permute-start.1 = (bf16[2,128,128]{2,1,0:T(8,128)(2,1)S(1)}, bf16[2,128,128]{2,1,0:T(8,128)(2,1)S(1)}, u32[]{:S(2)}, u32[]{:S(2)}) collective-permute-start(bf16[2,128,128]{2,1,0:T(8,128)(2,1)S(1)} %collective-permute-done), channel_id=1, source_target_pairs={{0,8},{8,16},{16,24},{24,32},{32,40},{40,48},{48,56},{56,64},{64,7... | collective-permute-start | bytes 196616 | tf_op jit(solution)/shard_map/ppermute | solution.py:315
  19.5 1.3 copy-start.2
  20.9 1.3 copy-start.4
  20.9 1.3 copy-start.5
  22.9 3.8 %collective-permute-start.2 = (bf16[2,128,128]{2,1,0:T(8,128)(2,1)S(1)}, bf16[2,128,128]{2,1,0:T(8,128)(2,1)S(1)}, u32[]{:S(2)}, u32[]{:S(2)}) collective-permute-start(bf16[2,128,128]{2,1,0:T(8,128)(2,1)S(1)} %collective-permute-done.1), channel_id=1, source_target_pairs={{0,8},{8,16},{16,24},{24,32},{32,40},{40,48},{48,56},{56,64},{64,7... | collective-permute-start | bytes 196616 | tf_op jit(solution)/shard_map/ppermute | solution.py:315
  26.7 5.6 %collective-permute-start.3 = (bf16[2,128,128]{2,1,0:T(8,128)(2,1)S(1)}, bf16[2,128,128]{2,1,0:T(8,128)(2,1)S(1)}, u32[]{:S(2)}, u32[]{:S(2)}) collective-permute-start(bf16[2,128,128]{2,1,0:T(8,128)(2,1)S(1)} %collective-permute-done.2), channel_id=1, source_target_pairs={{0,8},{8,16},{16,24},{24,32},{32,40},{40,48},{48,56},{56,64},{64,7... | collective-permute-start | bytes 196616 | tf_op jit(solution)/shard_map/ppermute | solution.py:315
  32.3 5.6 %collective-permute-start.4 = (bf16[2,128,128]{2,1,0:T(8,128)(2,1)S(1)}, bf16[2,128,128]{2,1,0:T(8,128)(2,1)S(1)}, u32[]{:S(2)}, u32[]{:S(2)}) collective-permute-start(bf16[2,128,128]{2,1,0:T(8,128)(2,1)S(1)} %collective-permute-done.3), channel_id=1, source_target_pairs={{0,8},{8,16},{16,24},{24,32},{32,40},{40,48},{48,56},{56,64},{64,7... | collective-permute-start | bytes 196616 | tf_op jit(solution)/shard_map/ppermute | solution.py:315
  37.9 5.6 %collective-permute-start.5 = (bf16[2,128,128]{2,1,0:T(8,128)(2,1)S(1)}, bf16[2,128,128]{2,1,0:T(8,128)(2,1)S(1)}, u32[]{:S(2)}, u32[]{:S(2)}) collective-permute-start(bf16[2,128,128]{2,1,0:T(8,128)(2,1)S(1)} %collective-permute-done.4), channel_id=1, source_target_pairs={{0,8},{8,16},{16,24},{24,32},{32,40},{40,48},{48,56},{56,64},{64,7... | collective-permute-start | bytes 196616 | tf_op jit(solution)/shard_map/ppermute | solution.py:315
  43.5 5.6 %collective-permute-start.6 = (bf16[2,128,128]{2,1,0:T(8,128)(2,1)S(1)}, bf16[2,128,128]{2,1,0:T(8,128)(2,1)}, u32[]{:S(2)}, u32[]{:S(2)}) collective-permute-start(bf16[2,128,128]{2,1,0:T(8,128)(2,1)S(1)} %collective-permute-done.5), channel_id=1, source_target_pairs={{0,8},{8,16},{16,24},{24,32},{32,40},{40,48},{48,56},{56,64},{64,7... | collective-permute-start | bytes 196616 | tf_op jit(solution)/shard_map/ppermute | solution.py:315
  49.0 6.0 %collective-permute-start.7 = (bf16[2,128,128]{2,1,0:T(8,128)(2,1)}, bf16[2,128,128]{2,1,0:T(8,128)(2,1)S(1)}, u32[]{:S(2)}, u32[]{:S(2)}) collective-permute-start(bf16[2,128,128]{2,1,0:T(8,128)(2,1)} %collective-permute-done.6), channel_id=1, source_target_pairs={{0,8},{8,16},{16,24},{24,32},{32,40},{40,48},{48,56},{56,64},{64,7... | collective-permute-start | bytes 196616 | tf_op jit(solution)/shard_map/ppermute | solution.py:315
  55.2 1.0 copy-start.3
  56.4 13.4 %copy-start = (bf16[128,1024]{1,0:T(8,128)(2,1)}, bf16[128,1024]{1,0:T(8,128)(2,1)S(1)}, u32[]{:S(2)}) copy-start(bf16[128,1024]{1,0:T(8,128)(2,1)S(1)} %get-tuple-element.428) | copy-start | bytes 786436

commit v2 on v1

--- a/solution.py
+++ b/solution.py
@@ -42,9 +42,22 @@
 FIRST = 4
 
 
-def ffn_kernel(
-    normed_ref, gate_ref, up_ref, out_ref,
+def document_starts(lengths_ref, positions):
+    starts = jnp.zeros_like(positions)
+    end = jnp.int32(0)
+    for i in range(lengths_ref.shape[0]):
+        end = end + lengths_ref[i]
+        starts = jnp.where(positions >= end, end, starts)
+    return starts
+
+
+def layer_kernel(
+    lengths_ref, query_ref, key_ref, value_ref, residual_in_ref, gain_ref, gate_ref, up_ref,
+    residual_ref, out_ref,
     tokens, weights, staged, landed, own_sum,
+    query, by_head, keys_values, residual_in, tails, normed_ref, squares,
+    running_max, denominator, weighted,
+    load_sem, kv_send, kv_sib_send, kv_recv, sq_send, sq_recv,
     w_send, w_recv, cross_send, tok_recv, up_send, down_send, sib_send, hi_send, sum_send, sum_recv,
 ):
     yh, z, c, x, yl = place()
@@ -59,17 +72,70 @@
     x_peers = [device(yh, z, c, lax.rem(x + d, 4), yl) for d in (1, 2, 3)]
     mine = pl.ds(pl.multiple_of(c * ROWS, ROWS), ROWS)
 
+    mp = x * 2 + yl
+    chip = yh * 8 + z
+    after = device(lax.rem((chip + 1) // 8, 2), lax.rem(chip + 1, 8), c, x, yl)
+    before = device(lax.rem((chip + 15) // 8, 2), lax.rem(chip + 15, 8), c, x, yl)
+
+    loads = [
+        pltpu.make_async_copy(key_ref, keys_values.at[0, 0, mine], load_sem.at[0]),
+        pltpu.make_async_copy(value_ref, keys_values.at[0, 1, mine], load_sem.at[1]),
+        pltpu.make_async_copy(query_ref, query, load_sem.at[2]),
+        pltpu.make_async_copy(residual_in_ref, residual_in, load_sem.at[3]),
+        pltpu.make_async_copy(gate_ref.at[:, pl.ds(0, 256)], weights.at[yl, :, pl.ds(0, 256)], load_sem.at[4]),
+        pltpu.make_async_copy(up_ref.at[:, pl.ds(0, 256)], weights.at[yl, :, pl.ds(256, 256)], load_sem.at[5]),
+        pltpu.make_async_copy(gate_ref.at[:, pl.ds(256, 128)], weights.at[yl, :, pl.ds(512, 128)], load_sem.at[6]),
+        pltpu.make_async_copy(up_ref.at[:, pl.ds(256, 128)], weights.at[yl, :, pl.ds(640, 128)], load_sem.at[7]),
+        pltpu.make_async_copy(gate_ref.at[:, pl.ds(384, 64)], tails.at[0], load_sem.at[8]),
+        pltpu.make_async_copy(up_ref.at[:, pl.ds(384, 64)], tails.at[1], load_sem.at[9]),
+    ]
+    for load in loads:
+        load.start()
+
     barrier = pltpu.get_barrier_semaphore()
-    peers = [sibling, lo_partner, hi_partner, above, below] + x_peers
+    across = [device(yh, z, c, lax.rem(x + d, 4), 1 - yl) for d in (1, 2, 3)]
+    peers = [sibling, lo_partner, hi_partner, above, below] + x_peers + across
     for peer in peers:
         pl.semaphore_signal(barrier, inc=1, device_id=peer, device_id_type=MESH)
 
-    weights[yl, :, 0:256] = gate_ref[:, 0:256]
-    weights[yl, :, 256:512] = up_ref[:, 0:256]
-    weights[yl, :, 512:640] = gate_ref[:, 256:384]
-    weights[yl, :, 640:768] = up_ref[:, 256:384]
-    weights[yl, :, 768:896] = jnp.concatenate([gate_ref[:, 384:448], up_ref[:, 384:448]], axis=1)
-    pl.semaphore_wait(barrier, len(peers))
+    @pl.when(chip == 8)
+    def _():
+        pl.semaphore_signal(barrier, inc=1, device_id=before, device_id_type=MESH)
+
+    pl.semaphore_wait(barrier, len(peers) + jnp.where(chip == 7, 1, 0))
+    for load in loads[:2]:
+        load.wait()
+
+    def kv_onward(j):
+        return pltpu.make_async_remote_copy(
+            src_ref=keys_values.at[j, :, mine], dst_ref=keys_values.at[j + 1, :, mine],
+            send_sem=kv_send.at[j], recv_sem=kv_recv.at[j + 1, c],
+            device_id=after, device_id_type=MESH,
+        )
+
+    def kv_sibling(j):
+        view = keys_values.at[j, :, mine]
+        return pltpu.make_async_remote_copy(
+            src_ref=view, dst_ref=view, send_sem=kv_sib_send.at[j], recv_sem=kv_recv.at[j, c],
+            device_id=sibling, device_id_type=MESH,
+        )
+
+    def kv_arrival(j, core):
+        view = keys_values.at[j, :, pl.ds(pl.multiple_of(core * ROWS, ROWS), ROWS)]
+        return pltpu.make_async_remote_copy(
+            src_ref=view, dst_ref=view, send_sem=kv_sib_send.at[j], recv_sem=kv_recv.at[j, core],
+            device_id=sibling, device_id_type=MESH,
+        )
+
+    @pl.when(chip < 15)
+    def _():
+        kv_onward(0).start()
+
+    kv_sibling(0).start()
+
+    for load in loads[4:]:
+        load.wait()
+    weights[yl, :, 768:896] = jnp.concatenate([tails[0], tails[1]], axis=1)
 
     def weight_copy(part):
         start, size = PARTS[part]
@@ -176,14 +242,6 @@
         for i in range(2):
             token_arrival(h, source, i, 1 - c).wait_recv()
 
-    @pl.when(match)
-    def _():
-        tokens[yh, my_source, yl, mine] = normed_ref[...]
-
-    @pl.when(jnp.logical_not(match))
-    def _():
-        cross_copy().start()
-
     for part in range(2):
         weight_copy(part).start()
 
@@ -194,6 +252,110 @@
             src_ref=view, dst_ref=view, send_sem=w_send.at[part], recv_sem=w_recv.at[part],
             device_id=lo_partner, device_id_type=MESH,
         ).wait_recv()
+
+    for load in loads[2:4]:
+        load.wait()
+    for head in range(8):
+        by_head[head // 2, (head % 2) * ROWS:(head % 2 + 1) * ROWS] = query[:, head * HD:(head + 1) * HD]
+    running_max[...] = jnp.full_like(running_max, -1e30)
+    denominator[...] = jnp.zeros_like(denominator)
+    weighted[...] = jnp.zeros_like(weighted)
+    query_pos = (chip * 2 + c) * ROWS + lax.broadcasted_iota(jnp.int32, (1, ROWS), 1)
+    starts = document_starts(lengths_ref, query_pos)
+
+    def attend(j):
+        key_pos = (chip - j) * 256 + lax.broadcasted_iota(jnp.int32, (256, ROWS), 0)
+        visible = jnp.logical_and(key_pos >= starts, key_pos <= query_pos)
+        bias = jnp.where(visible, 0.0, -1e30)
+        bias = jnp.concatenate([bias, bias], axis=1)
+
+        def pair(i, _):
+            scores = lax.dot_general(
+                keys_values[j, 0], by_head[i], (((1,), (1,)), ((), ())),
+                preferred_element_type=jnp.float32,
+            ) * HD ** (-0.5)
+            scores = jnp.where(bias < 0.0, -1e30, scores)
+            old = running_max[i]
+            new = jnp.maximum(old, jnp.max(scores, axis=0, keepdims=True))
+            factor = jnp.exp(old - new)
+            parts = jnp.exp(scores - new)
+            running_max[i] = new
+            denominator[i] = denominator[i] * factor + jnp.sum(parts, axis=0, keepdims=True)
+            weighted[i] = weighted[i] * factor + lax.dot_general(
+                keys_values[j, 1], parts.astype(jnp.bfloat16), (((0,), (0,)), ((), ())),
+                preferred_element_type=jnp.float32,
+            )
+            return 0
+
+        lax.fori_loop(0, 4, pair, 0)
+
+    def attend_step(j, _):
+        @pl.when(jnp.logical_and(j < 4, chip > j))
+        def _():
+            kv_arrival(j + 1, c).wait_recv()
+
+            @pl.when(jnp.logical_and(j < 3, chip < 15))
+            def _():
+                kv_onward(j + 1).start()
+
+            kv_sibling(j + 1).start()
+
+        @pl.when(jnp.logical_and(j < 4, chip <= j))
+        def _():
+            keys_values[j + 1] = jnp.zeros_like(keys_values[0])
+
+        @pl.when(chip >= j)
+        def _():
+            kv_arrival(j, 1 - c).wait_recv()
+
+        attend(j)
+        return 0
+
+    lax.fori_loop(0, 5, attend_step, 0)
+
+    total = jnp.zeros((ROWS, HD), jnp.float32)
+    for head in range(8):
+        lanes = slice((head % 2) * ROWS, (head % 2 + 1) * ROWS)
+        columns = slice(head * HD, (head + 1) * HD)
+        attended = (weighted[head // 2, :, lanes] / denominator[head // 2, :, lanes]).T
+        rounded = (residual_in[:, columns].astype(jnp.float32) + attended).astype(jnp.bfloat16)
+        residual_ref[:, columns] = rounded
+        wide = rounded.astype(jnp.float32)
+        total = total + wide * wide
+    squares[mp] = jnp.broadcast_to(jnp.sum(total.T, axis=0, keepdims=True), (8, ROWS))
+
+    def square_copy(peer, i):
+        view = squares.at[mp]
+        return pltpu.make_async_remote_copy(
+            src_ref=view, dst_ref=view, send_sem=sq_send.at[i], recv_sem=sq_recv.at[mp],
+            device_id=peer, device_id_type=MESH,
+        )
+
+    mp_peers = [lo_partner] + x_peers + across
+    for i, peer in enumerate(mp_peers):
+        square_copy(peer, i).start()
+    for i in range(1, 8):
+        slot = lax.rem(mp + i, 8)
+        view = squares.at[slot]
+        pltpu.make_async_remote_copy(
+            src_ref=view, dst_ref=view, send_sem=sq_send.at[0], recv_sem=sq_recv.at[slot],
+            device_id=lo_partner, device_id_type=MESH,
+        ).wait_recv()
+    mean = jnp.sum(squares[...], axis=0) / D
+    inverse = jnp.broadcast_to(lax.rsqrt(mean + 1e-05)[0:1], (ROWS, ROWS)).T
+    for head in range(8):
+        columns = slice(head * HD, (head + 1) * HD)
+        normed_ref[:, columns] = (
+            residual_ref[:, columns].astype(jnp.float32) * inverse * gain_ref[:, columns].astype(jnp.float32)
+        ).astype(jnp.bfloat16)
+
+    @pl.when(match)
+    def _():
+        tokens[yh, my_source, yl, mine] = normed_ref[...]
+
+    @pl.when(jnp.logical_not(match))
+    def _():
+        cross_copy().start()
 
     handle(0)
     weights_arrived(0)
@@ -251,6 +413,17 @@
 
     lax.fori_loop(0, 2, finish, 0)
 
+    for j in range(5):
+        if j < 4:
+            @pl.when(jnp.logical_and(chip < 15, chip >= j))
+            def _():
+                kv_onward(j).wait_send()
+
+        @pl.when(chip >= j)
+        def _():
+            kv_sibling(j).wait_send()
+    for i, peer in enumerate(mp_peers):
+        square_copy(peer, i).wait_send()
     for part in range(2):
         weight_copy(part).wait_send()
 
@@ -284,20 +457,37 @@
     lax.fori_loop(0, 8, drain, 0)
 
 
-def feed_forward(normed, gate_weight, up_weight):
+def on_device(
+    query_heads, key_heads, value_heads, residual_in, norm_gain, gate_weight, up_weight, doc_lengths
+):
     dma = pltpu.SemaphoreType.DMA
     vmem = pl.BlockSpec(memory_space=pltpu.VMEM)
+    anywhere = pl.BlockSpec(memory_space=pl.ANY)
     return pl.pallas_call(
-        ffn_kernel,
-        out_shape=jax.ShapeDtypeStruct((512, 448), jnp.bfloat16),
-        in_specs=[vmem] * 3,
-        out_specs=vmem,
+        layer_kernel,
+        out_shape=(
+            jax.ShapeDtypeStruct((ROWS, KB), jnp.bfloat16),
+            jax.ShapeDtypeStruct((512, 448), jnp.bfloat16),
+        ),
+        in_specs=[pl.BlockSpec(memory_space=pltpu.SMEM)] + [anywhere] * 4 + [vmem] + [anywhere] * 2,
+        out_specs=(vmem, vmem),
         scratch_shapes=[
             pltpu.VMEM((2, 4, 2, 2 * ROWS, KB), jnp.bfloat16),
             pltpu.VMEM((2, KB, WIDTH), jnp.bfloat16),
             pltpu.VMEM((2, 4, 2 * ROWS, WIDTH), jnp.bfloat16),
             pltpu.VMEM((3, 2, 2 * ROWS, WIDTH), jnp.bfloat16),
             pltpu.VMEM((2, 2 * ROWS, WIDTH), jnp.float32),
+            pltpu.VMEM((ROWS, KB), jnp.bfloat16),
+            pltpu.VMEM((4, 2 * ROWS, HD), jnp.bfloat16),
+            pltpu.VMEM((5, 2, 2 * ROWS, HD), jnp.bfloat16),
+            pltpu.VMEM((ROWS, KB), jnp.bfloat16),
+            pltpu.VMEM((2, KB, 64), jnp.bfloat16),
+            pltpu.VMEM((ROWS, KB), jnp.bfloat16),
+            pltpu.VMEM((8, 8, ROWS), jnp.float32),
+            pltpu.VMEM((4, 1, 2 * ROWS), jnp.float32),
+            pltpu.VMEM((4, 1, 2 * ROWS), jnp.float32),
+            pltpu.VMEM((4, HD, 2 * ROWS), jnp.float32),
+            dma((10,)), dma((4,)), dma((5,)), dma((5, 2)), dma((7,)), dma((8,)),
             dma((2,)), dma((2,)), dma((1,)), dma((2, 4, 2, 2)),
             dma((2, 4, 2)), dma((2, 4, 2)), dma((2, 4, 2)), dma((2, 4, 2)),
             dma((2, 4, 2)), dma((3, 2, 2)),
@@ -305,90 +495,11 @@
         compiler_params=pltpu.CompilerParams(
             collective_id=0, has_side_effects=True, vmem_limit_bytes=56 * 2**20
         ),
-        name="feed_forward",
-    )(normed, gate_weight, up_weight)
-
-
-def from_behind(block, axis, distance):
-    devices = range(lax.axis_size(axis))
-    route = [(i - distance, i) for i in devices if i - distance in devices]
-    return lax.ppermute(block, axis, route)
-
-
-def document_index(positions, doc_ends):
-    return jnp.sum((positions[:, None] >= doc_ends[None, :]).astype(jnp.int32), axis=1)
-
-
-def on_device(
-    query_heads, key_heads, value_heads, residual_in, norm_gain, gate_weight, up_weight, doc_lengths
-):
-    local_rows = query_heads.shape[0]
-    ctx_count = lax.axis_size("ctx")
-    ctx_index = lax.axis_index("ctx")
-    doc_ends = jnp.cumsum(doc_lengths)
-    query_pos = ctx_index * local_rows + jnp.arange(local_rows, dtype=jnp.int32)
-    query_doc = document_index(query_pos, doc_ends)
-    kv_groups = key_heads.shape[1] // HD
-    group_size = query_heads.shape[1] // HD // kv_groups
-    query_split = query_heads.reshape(local_rows, kv_groups, group_size, HD)
-
-    def attend(carried, key_piece, value_piece, offset):
-        key_count = key_piece.shape[0]
-        key_pos = offset + jnp.arange(key_count, dtype=jnp.int32)
-        key_doc = document_index(key_pos, doc_ends)
-        visible = (
-            (query_doc[:, None] == key_doc[None, :])
-            & (key_pos[None, :] <= query_pos[:, None])
-            & (key_pos[None, :] >= 0)
-        )
-
-        def update(previous):
-            running_max, denominator, weighted = previous
-            key_split = key_piece.reshape(key_count, kv_groups, HD)
-            value_split = value_piece.reshape(key_count, kv_groups, HD)
-            scores = jnp.einsum(
-                "qhgd,khd->hgqk", query_split, key_split, preferred_element_type=jnp.float32
-            ) * HD ** (-0.5)
-            scores = jnp.where(visible, scores, -1e30)
-            new_max = jnp.maximum(running_max, jnp.max(scores, axis=-1))
-            factor = jnp.exp(running_max - new_max)
-            weights = jnp.where(visible, jnp.exp(scores - new_max[..., None]), 0.0)
-            denominator = denominator * factor + jnp.sum(weights, axis=-1)
-            weighted = weighted * factor[..., None] + jnp.einsum(
-                "hgqk,khd->hgqd",
-                weights.astype(jnp.bfloat16),
-                value_split,
-                preferred_element_type=jnp.float32,
-            )
-            return (new_max, denominator, weighted)
-
-        return lax.cond(jnp.any(visible), update, lambda previous: previous, carried)
-
-    starting = (
-        jnp.full((kv_groups, group_size, local_rows), -1e30, jnp.float32),
-        jnp.zeros((kv_groups, group_size, local_rows), jnp.float32),
-        jnp.zeros((kv_groups, group_size, local_rows, HD), jnp.float32),
+        name="layer",
+    )(
+        doc_lengths, query_heads, key_heads, value_heads, residual_in,
+        norm_gain.reshape(1, KB), gate_weight, up_weight,
     )
-    finished = attend(starting, key_heads, value_heads, ctx_index * local_rows)
-    travelling = jnp.stack([key_heads, value_heads])
-    for distance in range(1, ctx_count // 4 + 1):
-        travelling = from_behind(travelling, "ctx", 1)
-        finished = attend(
-            finished, travelling[0], travelling[1], (ctx_index - distance) * local_rows
-        )
-    running_max, denominator, weighted = finished
-    attended = jnp.transpose(weighted / denominator[..., None], (2, 0, 1, 3)).reshape(
-        local_rows, kv_groups * group_size * HD
-    )
-    residual = (residual_in.astype(jnp.float32) + attended).astype(jnp.bfloat16)
-    residual_float = residual.astype(jnp.float32)
-    squares = lax.psum(jnp.sum(residual_float * residual_float, axis=1), "mp")
-    inverse = lax.rsqrt(squares / D + 1e-05)
-    normed = (residual_float * inverse[:, None] * norm_gain.astype(jnp.float32)[None, :]).astype(
-        jnp.bfloat16
-    )
-    hidden = feed_forward(normed, gate_weight, up_weight)
-    return (residual, hidden)
 
 
 def solution(mesh):

time: 238 us -> 169 us (0.71)
  the two profiles are of different devices: /device:TPU:39 before, /device:TPU:38 now
where the time goes in v2:
time: 169 us
  Pallas kernels  161 us (95%)
  local copies, waits for them, and re-layouts  7.66 us (5%)
    pallas_call x1, Pallas kernels, on_device(): pl.pallas_call(layer_kernel, out_shape=(jax.ShapeDtypeStruct((ROWS, KB),...  161 us
    unnamed x7, local copies, waits for them, and re-layouts  4.34 us

profile of v2, /device:TPU:38, one launch (start us, length us, event | category | flops | bytes accessed | tf_op | source)
XLA Modules:
  0.0 169.3 jit_solution(5186134750244599767)
XLA Ops:
  0.6 1.3 reshape.7.gain_ref
  1.9 0.0 copy-start
  1.9 2.3 %copy.10.gate_ref = bf16[1024,448]{1,0:T(8,128)(2,1)} copy(bf16[1024,448]{0,1:T(8,128)(2,1)} %param.13) | data formatting | bytes 1835008 | tf_op args[5]
  4.2 0.0 copy-done
  4.2 1.3 copy.11.up_ref
  5.5 161.0 %layer.1 = (bf16[128,1024]{1,0:T(8,128)(2,1)}, bf16[512,448]{1,0:T(8,128)(2,1)}) custom-call(s32[16]{0:T(128)} %lengths_ref.1, bf16[128,1024]{1,0:T(8,128)(2,1)} %query_ref.1, bf16[128,128]{1,0:T(8,128)(2,1)} %key_ref.1, bf16[128,128]{1,0:T(8,128)(2,1)} %value_ref.1, bf16[128,1024]{1,0:T(8,128)(2,1)} %residual_in_ref.1, bf16[1,1024]{1,0:T(2,128)(2,1)} %reshape.7.gain_ref, ...), custom_call_target="tpu_custom_call" | custom-call | tf_op jit(solution)/shard_map/layer/pallas_call | solution.py:466
  166.5 0.0 copy-start.1
  166.5 2.0 %copy.12 = bf16[512,448]{0,1:T(8,128)(2,1)} copy(bf16[512,448]{1,0:T(8,128)(2,1)} %get-tuple-element.3) | data formatting | bytes 917504 | tf_op jit(solution)/shard_map/layer/pallas_call | solution.py:466
  168.6 0.0 copy-done.1
  168.6 0.7 copy.14
Async XLA Ops:
  1.9 2.3 %copy-start = (bf16[1024,448]{0,1:T(8,128)(2,1)S(1)}, bf16[1024,448]{0,1:T(8,128)(2,1)}, u32[]{:S(2)}) copy-start(bf16[1024,448]{0,1:T(8,128)(2,1)} %param.14) | copy-start | bytes 2752516
  166.5 2.1 %copy-start.1 = (bf16[128,1024]{1,0:T(8,128)(2,1)S(1)}, bf16[128,1024]{1,0:T(8,128)(2,1)}, u32[]{:S(2)}) copy-start(bf16[128,1024]{1,0:T(8,128)(2,1)} %get-tuple-element.6) | copy-start | bytes 786436

commit v3 on v2

--- a/solution.py
+++ b/solution.py
@@ -12,10 +12,8 @@
 MESH = pl.DeviceIdType.MESH
 ROWS = 128
 KB = 1024
-WIDTH_A = 512
-WIDTH_B = 384
-PARTS = ((0, WIDTH_A), (WIDTH_A, WIDTH_B))
-WIDTH = WIDTH_A + WIDTH_B
+HALF = 448
+WIDTH = 2 * HALF
 
 
 def place():
@@ -38,7 +36,7 @@
 OFFSETS = ((0, 0, -1, 1), (1, -1, 2, -2), (-3, 3, -2, 2), (4, -4, 3, -3))
 ONWARD_UP = ((1, 1, 1, 0), (0, 1, 0, 1), (1, 0, 1, 0), (0, 0, 0, 0))
 ONWARD_DOWN = ((1, 1, 0, 1), (1, 0, 1, 0), (0, 1, 0, 1), (0, 0, 0, 0))
-ORDER = ((0, 0), (1, 0), (2, 0), (0, 1), (3, 0), (1, 1), (2, 1), (3, 1))
+ORDER = ((0, 0), (1, 0), (0, 1), (1, 1), (2, 0), (2, 1), (3, 0), (3, 1))
 FIRST = 4
 
 
@@ -54,11 +52,11 @@
 def layer_kernel(
     lengths_ref, query_ref, key_ref, value_ref, residual_in_ref, gain_ref, gate_ref, up_ref,
     residual_ref, out_ref,
-    tokens, weights, staged, landed, own_sum,
-    query, by_head, keys_values, residual_in, tails, normed_ref, squares,
+    tokens, weights, staged, relayed, landed, own_sum,
+    query, by_head, keys_values, residual_in, normed_ref, squares,
     running_max, denominator, weighted,
     load_sem, kv_send, kv_sib_send, kv_recv, sq_send, sq_recv,
-    w_send, w_recv, cross_send, tok_recv, up_send, down_send, sib_send, hi_send, sum_send, sum_recv,
+    w_send, w_recv, cross_send, tok_recv, up_send, down_send, sib_send, hi_send, relay_send, relay_recv, sum_send, sum_recv,
 ):
     yh, z, c, x, yl = place()
     match = lax.rem(z // 2, 2) == yl
@@ -74,20 +72,16 @@
 
     mp = x * 2 + yl
     chip = yh * 8 + z
-    after = device(lax.rem((chip + 1) // 8, 2), lax.rem(chip + 1, 8), c, x, yl)
-    before = device(lax.rem((chip + 15) // 8, 2), lax.rem(chip + 15, 8), c, x, yl)
+    step_on = lambda k: device(lax.rem((chip + 16 + k) // 8, 2), lax.rem(chip + 16 + k, 8), c, x, yl)
+    after, after_two = step_on(1), step_on(2)
 
     loads = [
         pltpu.make_async_copy(key_ref, keys_values.at[0, 0, mine], load_sem.at[0]),
         pltpu.make_async_copy(value_ref, keys_values.at[0, 1, mine], load_sem.at[1]),
         pltpu.make_async_copy(query_ref, query, load_sem.at[2]),
         pltpu.make_async_copy(residual_in_ref, residual_in, load_sem.at[3]),
-        pltpu.make_async_copy(gate_ref.at[:, pl.ds(0, 256)], weights.at[yl, :, pl.ds(0, 256)], load_sem.at[4]),
-        pltpu.make_async_copy(up_ref.at[:, pl.ds(0, 256)], weights.at[yl, :, pl.ds(256, 256)], load_sem.at[5]),
-        pltpu.make_async_copy(gate_ref.at[:, pl.ds(256, 128)], weights.at[yl, :, pl.ds(512, 128)], load_sem.at[6]),
-        pltpu.make_async_copy(up_ref.at[:, pl.ds(256, 128)], weights.at[yl, :, pl.ds(640, 128)], load_sem.at[7]),
-        pltpu.make_async_copy(gate_ref.at[:, pl.ds(384, 64)], tails.at[0], load_sem.at[8]),
-        pltpu.make_async_copy(up_ref.at[:, pl.ds(384, 64)], tails.at[1], load_sem.at[9]),
+        pltpu.make_async_copy(gate_ref, weights.at[yl, pl.ds(0, HALF)], load_sem.at[4]),
+        pltpu.make_async_copy(up_ref, weights.at[yl, pl.ds(HALF, HALF)], load_sem.at[5]),
     ]
     for load in loads:
         load.start()
@@ -100,17 +94,23 @@
 
     @pl.when(chip == 8)
     def _():
-        pl.semaphore_signal(barrier, inc=1, device_id=before, device_id_type=MESH)
-
-    pl.semaphore_wait(barrier, len(peers) + jnp.where(chip == 7, 1, 0))
+        pl.semaphore_signal(barrier, inc=1, device_id=step_on(-1), device_id_type=MESH)
+
+    @pl.when(chip >= 2)
+    def _():
+        pl.semaphore_signal(barrier, inc=1, device_id=step_on(-2), device_id_type=MESH)
+
+    pl.semaphore_wait(
+        barrier, len(peers) + jnp.where(chip == 7, 1, 0) + jnp.where(chip <= 13, 1, 0)
+    )
     for load in loads[:2]:
         load.wait()
 
-    def kv_onward(j):
-        return pltpu.make_async_remote_copy(
-            src_ref=keys_values.at[j, :, mine], dst_ref=keys_values.at[j + 1, :, mine],
-            send_sem=kv_send.at[j], recv_sem=kv_recv.at[j + 1, c],
-            device_id=after, device_id_type=MESH,
+    def kv_onward(i, j, ahead, target):
+        return pltpu.make_async_remote_copy(
+            src_ref=keys_values.at[j, :, mine], dst_ref=keys_values.at[j + ahead, :, mine],
+            send_sem=kv_send.at[i], recv_sem=kv_recv.at[j + ahead, c],
+            device_id=target, device_id_type=MESH,
         )
 
     def kv_sibling(j):
@@ -129,21 +129,25 @@
 
     @pl.when(chip < 15)
     def _():
-        kv_onward(0).start()
+        kv_onward(0, 0, 1, after).start()
+
+    @pl.when(chip < 14)
+    def _():
+        kv_onward(1, 0, 2, after_two).start()
 
     kv_sibling(0).start()
 
     for load in loads[4:]:
         load.wait()
-    weights[yl, :, 768:896] = jnp.concatenate([tails[0], tails[1]], axis=1)
 
     def weight_copy(part):
-        start, size = PARTS[part]
-        view = weights.at[yl, :, pl.ds(start, size)]
+        view = weights.at[yl, pl.ds(part * HALF, HALF)]
         return pltpu.make_async_remote_copy(
             src_ref=view, dst_ref=view, send_sem=w_send.at[part], recv_sem=w_recv.at[part],
             device_id=lo_partner, device_id_type=MESH,
         )
+
+    weight_copy(0).start()
 
     def cross_copy():
         return pltpu.make_async_remote_copy(
@@ -205,49 +209,79 @@
             def _():
                 token_copy(h, source, kb, hi_send, hi_partner).start()
 
-    def sum_copy(h, source, part, peer):
-        start, size = PARTS[part]
+    def role_of(h, source):
+        return lax.rem(x - (h * 2 + source // 2) + 4, 4)
+
+    def goes_up(source, part):
+        return lax.rem(source + part, 2) == 0
+
+    def sum_copy(h, source, part):
+        rows = pl.ds(part * HALF, HALF)
+        slot = role_of(h, source) // 2
         low = lax.rem(source, 2)
-        owner = h * 2 + source // 2
-        slot = lax.rem(x - owner + 4, 4) - 1
-        return pltpu.make_async_remote_copy(
-            src_ref=staged.at[h, source, :, pl.ds(start, size)],
-            dst_ref=landed.at[slot, low, :, pl.ds(start, size)],
+        return pltpu.make_async_remote_copy(
+            src_ref=staged.at[h, source, rows], dst_ref=landed.at[slot, low, rows],
             send_sem=sum_send.at[h, source, part], recv_sem=sum_recv.at[slot, low, part],
-            device_id=device(yh, z, c, owner, yl), device_id_type=MESH,
-        )
+            device_id=device(yh, z, c, h * 2 + source // 2, yl), device_id_type=MESH,
+        )
+
+    def relay_copy(h, source, part):
+        towards = lax.rem(x + jnp.where(goes_up(source, part), 1, 3), 4)
+        return pltpu.make_async_remote_copy(
+            src_ref=staged.at[h, source, pl.ds(part * HALF, HALF)], dst_ref=relayed.at[h, source],
+            send_sem=relay_send.at[h, source, part], recv_sem=relay_recv.at[h, source],
+            device_id=device(yh, z, c, towards, yl), device_id_type=MESH,
+        )
+
+    def relays(role, source, part):
+        return jnp.logical_and(lax.rem(role, 2) == 1, (role == 3) == goes_up(source, part))
 
     def multiply(step, part):
         h, _, source, _, _, _ = unit_of(step)
-        start, size = PARTS[part]
-        columns = pl.ds(start, size)
-        product = jnp.dot(
-            tokens[h, source, 0], weights[0, :, columns], preferred_element_type=jnp.float32
-        ) + jnp.dot(
-            tokens[h, source, 1], weights[1, :, columns], preferred_element_type=jnp.float32
-        )
-        owned = h * 2 + source // 2 == x
-
-        @pl.when(owned)
-        def _():
-            own_sum[lax.rem(source, 2), :, columns] = product
-
-        @pl.when(jnp.logical_not(owned))
-        def _():
-            staged[h, source, :, columns] = product.astype(jnp.bfloat16)
-            sum_copy(h, source, part, None).start()
+        rows = pl.ds(part * HALF, HALF)
+        across_k = (((1,), (1,)), ((), ()))
+        product = lax.dot_general(
+            weights[0, rows], tokens[h, source, 0], across_k, preferred_element_type=jnp.float32
+        ) + lax.dot_general(
+            weights[1, rows], tokens[h, source, 1], across_k, preferred_element_type=jnp.float32
+        )
+        role = role_of(h, source)
+
+        @pl.when(role == 0)
+        def _():
+            own_sum[lax.rem(source, 2), rows] = product
+
+        @pl.when(role != 0)
+        def _():
+            staged[h, source, rows] = product.astype(jnp.bfloat16)
+
+        @pl.when(role == 2)
+        def _():
+            relay_copy(h, source, part).start()
+
+        @pl.when(jnp.logical_and(lax.rem(role, 2) == 1, jnp.logical_not(relays(role, source, part))))
+        def _():
+            sum_copy(h, source, part).start()
+
+    def add_relayed(step, part):
+        h, _, source, _, _, _ = unit_of(step)
+        rows = pl.ds(part * HALF, HALF)
+
+        @pl.when(relays(role_of(h, source), source, part))
+        def _():
+            relay_copy(h, source, part).wait_recv()
+            staged[h, source, rows] = (
+                staged[h, source, rows].astype(jnp.float32) + relayed[h, source].astype(jnp.float32)
+            ).astype(jnp.bfloat16)
+            sum_copy(h, source, part).start()
 
     def sibling_arrived(step):
         h, _, source, _, _, _ = unit_of(step)
         for i in range(2):
             token_arrival(h, source, i, 1 - c).wait_recv()
 
-    for part in range(2):
-        weight_copy(part).start()
-
     def weights_arrived(part):
-        start, size = PARTS[part]
-        view = weights.at[1 - yl, :, pl.ds(start, size)]
+        view = weights.at[1 - yl, pl.ds(part * HALF, HALF)]
         pltpu.make_async_remote_copy(
             src_ref=view, dst_ref=view, send_sem=w_send.at[part], recv_sem=w_recv.at[part],
             device_id=lo_partner, device_id_type=MESH,
@@ -294,9 +328,9 @@
         def _():
             kv_arrival(j + 1, c).wait_recv()
 
-            @pl.when(jnp.logical_and(j < 3, chip < 15))
-            def _():
-                kv_onward(j + 1).start()
+            @pl.when(jnp.logical_and(j < 2, chip < 14))
+            def _():
+                kv_onward(j + 2, j + 1, 2, after_two).start()
 
             kv_sibling(j + 1).start()
 
@@ -346,7 +380,7 @@
     for head in range(8):
         columns = slice(head * HD, (head + 1) * HD)
         normed_ref[:, columns] = (
-            residual_ref[:, columns].astype(jnp.float32) * inverse * gain_ref[:, columns].astype(jnp.float32)
+            residual_ref[:, columns].astype(jnp.float32) * inverse * gain_ref[columns].astype(jnp.float32)[None, :]
         ).astype(jnp.bfloat16)
 
     @pl.when(match)
@@ -358,12 +392,18 @@
         cross_copy().start()
 
     handle(0)
+    weight_copy(1).start()
     weights_arrived(0)
 
     def first(step, _):
         handle(step + 1)
         sibling_arrived(step)
         multiply(step, 0)
+
+        @pl.when(step > 0)
+        def _():
+            add_relayed(step - 1, 0)
+
         return 0
 
     lax.fori_loop(0, FIRST, first, 0)
@@ -374,6 +414,13 @@
         return 0
 
     lax.fori_loop(0, FIRST, catch_up, 0)
+    add_relayed(FIRST - 1, 0)
+
+    def catch_up_relayed(step, _):
+        add_relayed(step, 1)
+        return 0
+
+    lax.fori_loop(0, FIRST - 1, catch_up_relayed, 0)
 
     def second(step, _):
         @pl.when(step < 7)
@@ -381,44 +428,41 @@
             handle(step + 1)
 
         sibling_arrived(step)
-        multiply(step, 0)
-        multiply(step, 1)
+        for part in range(2):
+            multiply(step, part)
+
+        @pl.when(step > FIRST)
+        def _():
+            add_relayed(step - 1, 0)
+
+        add_relayed(step - 1, 1)
         return 0
 
     lax.fori_loop(FIRST, 8, second, 0)
-
-    def finish(low, _):
-        rows = pl.ds(pl.multiple_of(low * 256, 256), 256)
+    for part in range(2):
+        add_relayed(7, part)
+
+    for low in range(2):
         totals = []
         for part in range(2):
-            start, size = PARTS[part]
-            columns = pl.ds(start, size)
-            total = own_sum[low, :, columns]
-            for slot in range(3):
-                view = landed.at[slot, low, :, columns]
+            rows = pl.ds(part * HALF, HALF)
+            total = own_sum[low, rows]
+            for slot in range(2):
+                view = landed.at[slot, low, rows]
                 pltpu.make_async_remote_copy(
                     src_ref=view, dst_ref=view, send_sem=sum_send.at[0, 0, part],
                     recv_sem=sum_recv.at[slot, low, part], device_id=x_peers[0], device_id_type=MESH,
                 ).wait_recv()
-                total = total + landed[slot, low, :, columns].astype(jnp.float32)
+                total = total + landed[slot, low, rows].astype(jnp.float32)
             totals.append(total)
-        a, b = totals
-        silu = lambda v: v / (1.0 + jnp.exp(-v))
-        out_ref[rows, 0:256] = (silu(a[:, :256]) * a[:, 256:]).astype(jnp.bfloat16)
-        out_ref[rows, 256:384] = (silu(b[:, :128]) * b[:, 128:256]).astype(jnp.bfloat16)
-        tail = b[:, 256:384]
-        mixed = silu(tail) * pltpu.roll(tail, 64, 1)
-        out_ref[rows, 384:448] = mixed[:, :64].astype(jnp.bfloat16)
-        return 0
-
-    lax.fori_loop(0, 2, finish, 0)
-
+        gate, up = totals
+        out_ref[:, low * 256:(low + 1) * 256] = (gate / (1.0 + jnp.exp(-gate)) * up).astype(jnp.bfloat16)
+
+    for i, j, ahead, target in ((0, 0, 1, after), (1, 0, 2, after_two), (2, 1, 2, after_two), (3, 2, 2, after_two)):
+        @pl.when(jnp.logical_and(chip < 16 - ahead, chip >= j))
+        def _():
+            kv_onward(i, j, ahead, target).wait_send()
     for j in range(5):
-        if j < 4:
-            @pl.when(jnp.logical_and(chip < 15, chip >= j))
-            def _():
-                kv_onward(j).wait_send()
-
         @pl.when(chip >= j)
         def _():
             kv_sibling(j).wait_send()
@@ -448,10 +492,15 @@
             def _():
                 token_copy(h, source, kb, hi_send, hi_partner).wait_send()
 
-        @pl.when(h * 2 + source // 2 != x)
-        def _():
-            for part in range(2):
-                sum_copy(h, source, part, None).wait_send()
+        role = role_of(h, source)
+        for part in range(2):
+            @pl.when(role == 2)
+            def _():
+                relay_copy(h, source, part).wait_send()
+
+            @pl.when(lax.rem(role, 2) == 1)
+            def _():
+                sum_copy(h, source, part).wait_send()
         return 0
 
     lax.fori_loop(0, 8, drain, 0)
@@ -463,34 +512,34 @@
     dma = pltpu.SemaphoreType.DMA
     vmem = pl.BlockSpec(memory_space=pltpu.VMEM)
     anywhere = pl.BlockSpec(memory_space=pl.ANY)
-    return pl.pallas_call(
+    residual, hidden = pl.pallas_call(
         layer_kernel,
         out_shape=(
             jax.ShapeDtypeStruct((ROWS, KB), jnp.bfloat16),
-            jax.ShapeDtypeStruct((512, 448), jnp.bfloat16),
+            jax.ShapeDtypeStruct((HALF, 4 * ROWS), jnp.bfloat16),
         ),
         in_specs=[pl.BlockSpec(memory_space=pltpu.SMEM)] + [anywhere] * 4 + [vmem] + [anywhere] * 2,
         out_specs=(vmem, vmem),
         scratch_shapes=[
             pltpu.VMEM((2, 4, 2, 2 * ROWS, KB), jnp.bfloat16),
-            pltpu.VMEM((2, KB, WIDTH), jnp.bfloat16),
-            pltpu.VMEM((2, 4, 2 * ROWS, WIDTH), jnp.bfloat16),
-            pltpu.VMEM((3, 2, 2 * ROWS, WIDTH), jnp.bfloat16),
-            pltpu.VMEM((2, 2 * ROWS, WIDTH), jnp.float32),
+            pltpu.VMEM((2, WIDTH, KB), jnp.bfloat16),
+            pltpu.VMEM((2, 4, WIDTH, 2 * ROWS), jnp.bfloat16),
+            pltpu.VMEM((2, 4, HALF, 2 * ROWS), jnp.bfloat16),
+            pltpu.VMEM((2, 2, WIDTH, 2 * ROWS), jnp.bfloat16),
+            pltpu.VMEM((2, WIDTH, 2 * ROWS), jnp.float32),
             pltpu.VMEM((ROWS, KB), jnp.bfloat16),
             pltpu.VMEM((4, 2 * ROWS, HD), jnp.bfloat16),
             pltpu.VMEM((5, 2, 2 * ROWS, HD), jnp.bfloat16),
             pltpu.VMEM((ROWS, KB), jnp.bfloat16),
-            pltpu.VMEM((2, KB, 64), jnp.bfloat16),
             pltpu.VMEM((ROWS, KB), jnp.bfloat16),
             pltpu.VMEM((8, 8, ROWS), jnp.float32),
             pltpu.VMEM((4, 1, 2 * ROWS), jnp.float32),
             pltpu.VMEM((4, 1, 2 * ROWS), jnp.float32),
             pltpu.VMEM((4, HD, 2 * ROWS), jnp.float32),
-            dma((10,)), dma((4,)), dma((5,)), dma((5, 2)), dma((7,)), dma((8,)),
+            dma((6,)), dma((4,)), dma((5,)), dma((5, 2)), dma((7,)), dma((8,)),
             dma((2,)), dma((2,)), dma((1,)), dma((2, 4, 2, 2)),
             dma((2, 4, 2)), dma((2, 4, 2)), dma((2, 4, 2)), dma((2, 4, 2)),
-            dma((2, 4, 2)), dma((3, 2, 2)),
+            dma((2, 4, 2)), dma((2, 4)), dma((2, 4, 2)), dma((2, 2, 2)),
         ],
         compiler_params=pltpu.CompilerParams(
             collective_id=0, has_side_effects=True, vmem_limit_bytes=56 * 2**20
@@ -498,8 +547,9 @@
         name="layer",
     )(
         doc_lengths, query_heads, key_heads, value_heads, residual_in,
-        norm_gain.reshape(1, KB), gate_weight, up_weight,
+        norm_gain, gate_weight.T, up_weight.T,
     )
+    return residual, hidden.T
 
 
 def solution(mesh):

time: 169 us -> 129 us (0.76)
  the two profiles are of different devices: /device:TPU:38 before, /device:TPU:25 now
where the time goes in v3:
time: 129 us; the launch traced here: 126 us
  Pallas kernels  123 us (95%)
  local copies, waits for them, and re-layouts  2.49 us (2%)
    pallas_call x1, Pallas kernels, on_device(): pl.pallas_call(layer_kernel, out_shape=(jax.ShapeDtypeStruct((ROWS, KB),...  123 us

profile of v3, /device:TPU:25, one launch (start us, length us, event | category | flops | bytes accessed | tf_op | source)
XLA Modules:
  0.0 126.0 jit_solution(16715826266103919952)
XLA Ops:
  0.6 122.9 %layer.1 = (bf16[128,1024]{1,0:T(8,128)(2,1)}, bf16[448,512]{1,0:T(8,128)(2,1)}) custom-call(s32[16]{0:T(128)} %lengths_ref.1, bf16[128,1024]{1,0:T(8,128)(2,1)} %query_ref.1, bf16[128,128]{1,0:T(8,128)(2,1)} %key_ref.1, bf16[128,128]{1,0:T(8,128)(2,1)} %value_ref.1, bf16[128,1024]{1,0:T(8,128)(2,1)} %residual_in_ref.1, bf16[1024]{0:T(1024)(128)(2,1)} %gain_ref.1, ...), custom_call_target="tpu_custom_call" | custom-call | tf_op jit(solution)/shard_map/layer/pallas_call | solution.py:515
  123.5 0.0 copy-start
  123.5 1.7 %copy.12 = bf16[128,1024]{1,0:T(8,128)(2,1)} copy(bf16[128,1024]{1,0:T(8,128)(2,1)} %get-tuple-element.8) | data formatting | bytes 524288
  125.3 0.0 copy-done
  125.3 0.8 copy.13
Async XLA Ops:
  123.5 1.7 %copy-start = (bf16[448,512]{1,0:T(8,128)(2,1)S(1)}, bf16[448,512]{1,0:T(8,128)(2,1)}, u32[]{:S(2)}) copy-start(bf16[448,512]{1,0:T(8,128)(2,1)} %get-tuple-element.5) | copy-start | bytes 1376260

commit v4 on v3

--- a/solution.py
+++ b/solution.py
@@ -36,7 +36,15 @@
 OFFSETS = ((0, 0, -1, 1), (1, -1, 2, -2), (-3, 3, -2, 2), (4, -4, 3, -3))
 ONWARD_UP = ((1, 1, 1, 0), (0, 1, 0, 1), (1, 0, 1, 0), (0, 0, 0, 0))
 ONWARD_DOWN = ((1, 1, 0, 1), (1, 0, 1, 0), (0, 1, 0, 1), (0, 0, 0, 0))
-ORDER = ((0, 0), (1, 0), (0, 1), (1, 1), (2, 0), (2, 1), (3, 0), (3, 1))
+EVENTS = (
+    ((0, 0, 0), (0, 0, 1), (1, 0, 0), (0, 1, 0), (0, 1, 1), (1, 0, 1), (1, 1, 0), (2, 0, 0), (1, 1, 1), (2, 0, 1), (3, 0, 0), (2, 1, 0), (3, 0, 1), (2, 1, 1), (3, 1, 0), (3, 1, 1)),
+    ((0, 0, 0), (0, 0, 1), (1, 0, 0), (2, 0, 0), (1, 0, 1), (0, 1, 0), (0, 1, 1), (1, 1, 0), (2, 0, 1), (1, 1, 1), (2, 1, 0), (3, 0, 0), (2, 1, 1), (3, 0, 1), (3, 1, 0), (3, 1, 1)),
+)
+GROUPS = (
+    ((0, 0), (0, 1), (1, 0), (1, 1), (2, 0), (3, 0), (2, 1), (3, 1)),
+    ((0, 0), (1, 0), (0, 1), (2, 0), (1, 1), (2, 1), (3, 0), (3, 1)),
+)
+BEFORE = (3, 6, 8, 10, 11, 14, 15, 16)
 FIRST = 4
 
 
@@ -170,44 +178,46 @@
             recv_sem=tok_recv.at[h, source, kb, core], device_id=sibling, device_id_type=MESH,
         )
 
-    def unit_of(step):
-        unit = pick(step, [u for u, _ in ORDER])
-        half = pick(step, [h for _, h in ORDER])
+    def by_place(step, tables):
+        codes = [[u * 4 + sum(b << i for i, b in enumerate(rest)) for u, *rest in t] for t in tables]
+        code = jnp.where(w < 2, pick(step, codes[0]), pick(step, codes[1]))
+        return code // 4, lax.rem(code, 2), lax.rem(code // 2, 2)
+
+    def unit_of(unit, half):
         table = lambda rows: pick(unit * 4 + w, [v for row in rows for v in row])
         source_z = lax.rem(z + table(OFFSETS) + 8, 8)
         source = (source_z // 4) * 2 + lax.rem(source_z, 2)
-        h = lax.rem(yh + half, 2)
+        return lax.rem(yh + half, 2), source, table
+
+    def group_of(step):
+        unit, half, _ = by_place(step, GROUPS)
+        h, source, _ = unit_of(unit, half)
+        return h, source
+
+    def onward(unit, half, kb):
+        h, source, table = unit_of(unit, half)
         own = jnp.logical_and(match, unit == 0)
-        return h, half, source, own, table(ONWARD_UP) == 1, table(ONWARD_DOWN) == 1
-
-    def order_of_blocks(i):
-        return lax.rem(yl + i, 2)
-
-    def handle(step):
-        h, half, source, own, go_up, go_down = unit_of(step)
-        at_home = jnp.logical_and(own, half == 0)
-        for i in range(2):
-            kb = order_of_blocks(i)
-            if i == 0:
-                @pl.when(jnp.logical_not(at_home))
-                def _():
-                    token_arrival(h, source, kb, c).wait_recv()
-            else:
-                token_arrival(h, source, kb, c).wait_recv()
-
-            @pl.when(go_up)
+        return (
+            (table(ONWARD_UP) == 1, token_copy(h, source, kb, up_send, above)),
+            (table(ONWARD_DOWN) == 1, token_copy(h, source, kb, down_send, below)),
+            (unit >= 0, token_copy(h, source, kb, sib_send, sibling)),
+            (jnp.logical_and(own, half == 0), token_copy(h, source, kb, hi_send, hi_partner)),
+        )
+
+    def handle(event):
+        unit, half, block = by_place(event, EVENTS)
+        h, source, _ = unit_of(unit, half)
+        kb = lax.rem(yl + block, 2)
+        own = jnp.logical_and(match, unit == 0)
+
+        @pl.when(jnp.logical_not(jnp.logical_and(own, jnp.logical_and(half == 0, block == 0))))
+        def _():
+            token_arrival(h, source, kb, c).wait_recv()
+
+        for wanted, copy in onward(unit, half, kb):
+            @pl.when(wanted)
             def _():
-                token_copy(h, source, kb, up_send, above).start()
-
-            @pl.when(go_down)
-            def _():
-                token_copy(h, source, kb, down_send, below).start()
-
-            token_copy(h, source, kb, sib_send, sibling).start()
-
-            @pl.when(at_home)
-            def _():
-                token_copy(h, source, kb, hi_send, hi_partner).start()
+                copy.start()
 
     def role_of(h, source):
         return lax.rem(x - (h * 2 + source // 2) + 4, 4)
@@ -237,7 +247,7 @@
         return jnp.logical_and(lax.rem(role, 2) == 1, (role == 3) == goes_up(source, part))
 
     def multiply(step, part):
-        h, _, source, _, _, _ = unit_of(step)
+        h, source = group_of(step)
         rows = pl.ds(part * HALF, HALF)
         across_k = (((1,), (1,)), ((), ()))
         product = lax.dot_general(
@@ -264,7 +274,7 @@
             sum_copy(h, source, part).start()
 
     def add_relayed(step, part):
-        h, _, source, _, _, _ = unit_of(step)
+        h, source = group_of(step)
         rows = pl.ds(part * HALF, HALF)
 
         @pl.when(relays(role_of(h, source), source, part))
@@ -276,7 +286,7 @@
             sum_copy(h, source, part).start()
 
     def sibling_arrived(step):
-        h, _, source, _, _, _ = unit_of(step)
+        h, source = group_of(step)
         for i in range(2):
             token_arrival(h, source, i, 1 - c).wait_recv()
 
@@ -391,19 +401,23 @@
     def _():
         cross_copy().start()
 
-    handle(0)
-    weight_copy(1).start()
-    weights_arrived(0)
+    def handle_until(step):
+        def one(event, _):
+            handle(event)
+            return 0
+
+        lax.fori_loop(pick(step, (0,) + BEFORE[:-1]), pick(step, BEFORE), one, 0)
 
     def first(step, _):
-        handle(step + 1)
+        handle_until(step)
+
+        @pl.when(step == 0)
+        def _():
+            weight_copy(1).start()
+            weights_arrived(0)
+
         sibling_arrived(step)
         multiply(step, 0)
-
-        @pl.when(step > 0)
-        def _():
-            add_relayed(step - 1, 0)
-
         return 0
 
     lax.fori_loop(0, FIRST, first, 0)
@@ -414,33 +428,24 @@
         return 0
 
     lax.fori_loop(0, FIRST, catch_up, 0)
-    add_relayed(FIRST - 1, 0)
-
-    def catch_up_relayed(step, _):
-        add_relayed(step, 1)
-        return 0
-
-    lax.fori_loop(0, FIRST - 1, catch_up_relayed, 0)
 
     def second(step, _):
-        @pl.when(step < 7)
-        def _():
-            handle(step + 1)
-
+        handle_until(step)
         sibling_arrived(step)
         for part in range(2):
             multiply(step, part)
-
-        @pl.when(step > FIRST)
-        def _():
-            add_relayed(step - 1, 0)
-
-        add_relayed(step - 1, 1)
+        for part in range(2):
+            add_relayed(step - FIRST, part)
         return 0
 
     lax.fori_loop(FIRST, 8, second, 0)
-    for part in range(2):
-        add_relayed(7, part)
+
+    def last(step, _):
+        for part in range(2):
+            add_relayed(step, part)
+        return 0
+
+    lax.fori_loop(8 - FIRST, 8, last, 0)
 
     for low in range(2):
         totals = []
@@ -476,21 +481,13 @@
         cross_copy().wait_send()
 
     def drain(step, _):
-        h, half, source, own, go_up, go_down = unit_of(step)
+        unit, half = step // 2, lax.rem(step, 2)
+        h, source, _ = unit_of(unit, half)
         for kb in range(2):
-            @pl.when(go_up)
-            def _():
-                token_copy(h, source, kb, up_send, above).wait_send()
-
-            @pl.when(go_down)
-            def _():
-                token_copy(h, source, kb, down_send, below).wait_send()
-
-            token_copy(h, source, kb, sib_send, sibling).wait_send()
-
-            @pl.when(jnp.logical_and(own, half == 0))
-            def _():
-                token_copy(h, source, kb, hi_send, hi_partner).wait_send()
+            for wanted, copy in onward(unit, half, kb):
+                @pl.when(wanted)
+                def _():
+                    copy.wait_send()
 
         role = role_of(h, source)
         for part in range(2):

time: 129 us -> 115 us (0.89); the launches traced: 126 us -> 113 us
  Pallas kernels: 123 us -> 110 us
    pallas_call x1, Pallas kernels: 123 us -> 110 us  [on_device(): pl.pallas_call(layer_kernel, out_shape=(jax.ShapeDtypeStruct((ROWS, KB),...]
where the time goes in v4:
time: 115 us; the launch traced here: 113 us
  Pallas kernels  110 us (96%)
  local copies, waits for them, and re-layouts  2.49 us (2%)
    pallas_call x1, Pallas kernels, on_device(): pl.pallas_call(layer_kernel, out_shape=(jax.ShapeDtypeStruct((ROWS, KB),...  110 us
    unnamed x4, local copies, waits for them, and re-layouts  2.49 us

profile of v4, /device:TPU:25, one launch (start us, length us, event | category | flops | bytes accessed | tf_op | source)
XLA Modules:
  0.0 113.4 jit_solution(9108225643688667600)
XLA Ops:
  0.6 110.3 %layer.1 = (bf16[128,1024]{1,0:T(8,128)(2,1)}, bf16[448,512]{1,0:T(8,128)(2,1)}) custom-call(s32[16]{0:T(128)} %lengths_ref.1, bf16[128,1024]{1,0:T(8,128)(2,1)} %query_ref.1, bf16[128,128]{1,0:T(8,128)(2,1)} %key_ref.1, bf16[128,128]{1,0:T(8,128)(2,1)} %value_ref.1, bf16[128,1024]{1,0:T(8,128)(2,1)} %residual_in_ref.1, bf16[1024]{0:T(1024)(128)(2,1)} %gain_ref.1, ...), custom_call_target="tpu_custom_call" | custom-call | tf_op jit(solution)/shard_map/layer/pallas_call | solution.py:512
  110.9 0.0 copy-start
  110.9 1.7 %copy.12 = bf16[128,1024]{1,0:T(8,128)(2,1)} copy(bf16[128,1024]{1,0:T(8,128)(2,1)} %get-tuple-element.8) | data formatting | bytes 524288
  112.6 0.0 copy-done
  112.6 0.8 copy.13
Async XLA Ops:
  110.9 1.7 %copy-start = (bf16[448,512]{1,0:T(8,128)(2,1)S(1)}, bf16[448,512]{1,0:T(8,128)(2,1)}, u32[]{:S(2)}) copy-start(bf16[448,512]{1,0:T(8,128)(2,1)} %get-tuple-element.5) | copy-start | bytes 1376260

commit v5 on v4

--- a/solution.py
+++ b/solution.py
@@ -34,18 +34,28 @@
 
 
 OFFSETS = ((0, 0, -1, 1), (1, -1, 2, -2), (-3, 3, -2, 2), (4, -4, 3, -3))
-ONWARD_UP = ((1, 1, 1, 0), (0, 1, 0, 1), (1, 0, 1, 0), (0, 0, 0, 0))
-ONWARD_DOWN = ((1, 1, 0, 1), (1, 0, 1, 0), (0, 1, 0, 1), (0, 0, 0, 0))
+ONWARD_UP = (
+    ((1, 1, 1, 0), (0, 1, 0, 1), (1, 0, 1, 0), (0, 0, 0, 0)),
+    ((1, 1, 1, 0), (0, 1, 0, 1), (1, 0, 1, 0), (0, 0, 0, 0)),
+)
+ONWARD_DOWN = (
+    ((1, 1, 0, 1), (1, 0, 1, 0), (0, 1, 0, 1), (0, 0, 0, 0)),
+    ((1, 1, 0, 1), (1, 0, 1, 0), (0, 1, 0, 1), (0, 0, 0, 0)),
+)
+CROSSES = ((1, 1, 0, 0), (0, 0, 0, 0), (0, 0, 0, 0), (0, 0, 0, 0))
 EVENTS = (
-    ((0, 0, 0), (0, 0, 1), (1, 0, 0), (0, 1, 0), (0, 1, 1), (1, 0, 1), (1, 1, 0), (2, 0, 0), (1, 1, 1), (2, 0, 1), (3, 0, 0), (2, 1, 0), (3, 0, 1), (2, 1, 1), (3, 1, 0), (3, 1, 1)),
-    ((0, 0, 0), (0, 0, 1), (1, 0, 0), (2, 0, 0), (1, 0, 1), (0, 1, 0), (0, 1, 1), (1, 1, 0), (2, 0, 1), (1, 1, 1), (2, 1, 0), (3, 0, 0), (2, 1, 1), (3, 0, 1), (3, 1, 0), (3, 1, 1)),
+    ((0, 0, 0), (0, 0, 1), (1, 0, 0), (0, 1, 0), (0, 1, 1), (1, 0, 1), (2, 0, 0), (1, 1, 0), (2, 0, 1), (3, 0, 0), (1, 1, 1), (2, 1, 0), (3, 0, 1), (2, 1, 1), (3, 1, 0), (3, 1, 1)),
+    ((0, 0, 0), (0, 0, 1), (1, 0, 0), (2, 0, 0), (1, 0, 1), (0, 1, 0), (0, 1, 1), (1, 1, 0), (3, 0, 0), (1, 1, 1), (2, 0, 1), (2, 1, 0), (2, 1, 1), (3, 0, 1), (3, 1, 0), (3, 1, 1)),
 )
 GROUPS = (
-    ((0, 0), (0, 1), (1, 0), (1, 1), (2, 0), (3, 0), (2, 1), (3, 1)),
-    ((0, 0), (1, 0), (0, 1), (2, 0), (1, 1), (2, 1), (3, 0), (3, 1)),
+    ((0, 0), (0, 1), (1, 0), (2, 0), (1, 1), (3, 0), (2, 1), (3, 1)),
+    ((0, 0), (1, 0), (0, 1), (1, 1), (2, 0), (2, 1), (3, 0), (3, 1)),
 )
-BEFORE = (3, 6, 8, 10, 11, 14, 15, 16)
-FIRST = 4
+BEFORE = (3, 6, 8, 11, 12, 14, 15, 16)
+PIECES = ((0, 320, -1), (320, 128, 0), (448, 448, 0))
+GATED = (0, 0, 3, 4, 5, 6, 7, 8)
+UPPED = (0, 0, 0, 4, 5, 6, 7, 8)
+RELAYED = (0, 0, 0, 0, 1, 2, 3, 4)
 
 
 def document_starts(lengths_ref, positions):
@@ -61,9 +71,9 @@
     lengths_ref, query_ref, key_ref, value_ref, residual_in_ref, gain_ref, gate_ref, up_ref,
     residual_ref, out_ref,
     tokens, weights, staged, relayed, landed, own_sum,
-    query, by_head, keys_values, residual_in, normed_ref, squares,
+    query, by_head, keys_values, residual_in, scaled, squares, inverse,
     running_max, denominator, weighted,
-    load_sem, kv_send, kv_sib_send, kv_recv, sq_send, sq_recv,
+    load_sem, kv_send, kv_sib_send, kv_recv, sq_send, sq_recv, inv_send, inv_recv,
     w_send, w_recv, cross_send, tok_recv, up_send, down_send, sib_send, hi_send, relay_send, relay_recv, sum_send, sum_recv,
 ):
     yh, z, c, x, yl = place()
@@ -81,7 +91,7 @@
     mp = x * 2 + yl
     chip = yh * 8 + z
     step_on = lambda k: device(lax.rem((chip + 16 + k) // 8, 2), lax.rem(chip + 16 + k, 8), c, x, yl)
-    after, after_two = step_on(1), step_on(2)
+    kv_hops = ((0, 1, step_on(1)), (0, 2, step_on(2)), (0, 4, step_on(4)), (2, 1, step_on(1)))
 
     loads = [
         pltpu.make_async_copy(key_ref, keys_values.at[0, 0, mine], load_sem.at[0]),
@@ -104,23 +114,30 @@
     def _():
         pl.semaphore_signal(barrier, inc=1, device_id=step_on(-1), device_id_type=MESH)
 
-    @pl.when(chip >= 2)
-    def _():
-        pl.semaphore_signal(barrier, inc=1, device_id=step_on(-2), device_id_type=MESH)
+    for k in (2, 4):
+        @pl.when(chip >= k)
+        def _():
+            pl.semaphore_signal(barrier, inc=1, device_id=step_on(-k), device_id_type=MESH)
 
     pl.semaphore_wait(
-        barrier, len(peers) + jnp.where(chip == 7, 1, 0) + jnp.where(chip <= 13, 1, 0)
+        barrier,
+        len(peers) + jnp.where(chip == 7, 1, 0) + jnp.where(chip < 14, 1, 0) + jnp.where(chip < 12, 1, 0),
     )
     for load in loads[:2]:
         load.wait()
 
-    def kv_onward(i, j, ahead, target):
+    def kv_onward(i):
+        j, ahead, target = kv_hops[i]
         return pltpu.make_async_remote_copy(
             src_ref=keys_values.at[j, :, mine], dst_ref=keys_values.at[j + ahead, :, mine],
             send_sem=kv_send.at[i], recv_sem=kv_recv.at[j + ahead, c],
             device_id=target, device_id_type=MESH,
         )
 
+    def kv_sent(i):
+        j, ahead, _ = kv_hops[i]
+        return jnp.logical_and(chip >= j, chip < 16 - ahead)
+
     def kv_sibling(j):
         view = keys_values.at[j, :, mine]
         return pltpu.make_async_remote_copy(
@@ -135,31 +152,31 @@
             device_id=sibling, device_id_type=MESH,
         )
 
-    @pl.when(chip < 15)
-    def _():
-        kv_onward(0, 0, 1, after).start()
-
-    @pl.when(chip < 14)
-    def _():
-        kv_onward(1, 0, 2, after_two).start()
+    for i in range(3):
+        @pl.when(kv_sent(i))
+        def _():
+            kv_onward(i).start()
 
     kv_sibling(0).start()
 
     for load in loads[4:]:
         load.wait()
 
-    def weight_copy(part):
-        view = weights.at[yl, pl.ds(part * HALF, HALF)]
-        return pltpu.make_async_remote_copy(
-            src_ref=view, dst_ref=view, send_sem=w_send.at[part], recv_sem=w_recv.at[part],
+    def weight_copy(i):
+        start, rows, _ = PIECES[i]
+        view = weights.at[yl, pl.ds(start, rows)]
+        return pltpu.make_async_remote_copy(
+            src_ref=view, dst_ref=view, send_sem=w_send.at[i], recv_sem=w_recv.at[i],
             device_id=lo_partner, device_id_type=MESH,
         )
 
-    weight_copy(0).start()
+    for i, (_, _, when) in enumerate(PIECES):
+        if when < 0:
+            weight_copy(i).start()
 
     def cross_copy():
         return pltpu.make_async_remote_copy(
-            src_ref=normed_ref, dst_ref=tokens.at[yh, my_source, yl, mine],
+            src_ref=scaled, dst_ref=tokens.at[yh, my_source, yl, mine],
             send_sem=cross_send.at[0], recv_sem=tok_recv.at[yh, my_source, yl, c],
             device_id=lo_partner, device_id_type=MESH,
         )
@@ -194,15 +211,22 @@
         h, source, _ = unit_of(unit, half)
         return h, source
 
+    def ways_on(unit, half):
+        _, _, table = unit_of(unit, half)
+        by_half = lambda tables: jnp.where(half == 0, table(tables[0]), table(tables[1])) == 1
+        crosses = jnp.logical_and(table(CROSSES) == 1, half == 0)
+        return by_half(ONWARD_UP), by_half(ONWARD_DOWN), unit >= 0, crosses
+
     def onward(unit, half, kb):
-        h, source, table = unit_of(unit, half)
-        own = jnp.logical_and(match, unit == 0)
-        return (
-            (table(ONWARD_UP) == 1, token_copy(h, source, kb, up_send, above)),
-            (table(ONWARD_DOWN) == 1, token_copy(h, source, kb, down_send, below)),
-            (unit >= 0, token_copy(h, source, kb, sib_send, sibling)),
-            (jnp.logical_and(own, half == 0), token_copy(h, source, kb, hi_send, hi_partner)),
-        )
+        h, source, _ = unit_of(unit, half)
+        ways = ((up_send, above), (down_send, below), (sib_send, sibling), (hi_send, hi_partner))
+        return [
+            (wanted, token_copy(h, source, kb, sems, target))
+            for wanted, (sems, target) in zip(ways_on(unit, half), ways)
+        ]
+
+    def owned_here(h, source):
+        return h * 2 + source // 2 == x
 
     def handle(event):
         unit, half, block = by_place(event, EVENTS)
@@ -218,6 +242,24 @@
             @pl.when(wanted)
             def _():
                 copy.start()
+
+        @pl.when(jnp.logical_and(owned_here(h, source), block == 1))
+        def _():
+            low = lax.rem(source, 2)
+            at_home = jnp.logical_and(own, half == 0)
+
+            @pl.when(at_home)
+            def _():
+                squares_to_inverse()
+
+            @pl.when(jnp.logical_not(at_home))
+            def _():
+                inverse_copy(low, c, 0, sibling).wait_recv()
+
+            for wanted, copy in inverse_onward(ways_on(unit, half), low):
+                @pl.when(wanted)
+                def _():
+                    copy.start()
 
     def role_of(h, source):
         return lax.rem(x - (h * 2 + source // 2) + 4, 4)
@@ -290,12 +332,44 @@
         for i in range(2):
             token_arrival(h, source, i, 1 - c).wait_recv()
 
+    owner_mp = (yh * 2 + z // 4) * 2 + lax.rem(z // 2, 2)
+
+    def square_copy():
+        view = squares.at[mp]
+        return pltpu.make_async_remote_copy(
+            src_ref=view, dst_ref=view, send_sem=sq_send.at[0], recv_sem=sq_recv.at[mp],
+            device_id=(chip * 2 + c, owner_mp), device_id_type=MESH,
+        )
+
+    def squares_to_inverse():
+        for i in range(1, 8):
+            slot = lax.rem(mp + i, 8)
+            view = squares.at[slot]
+            pltpu.make_async_remote_copy(
+                src_ref=view, dst_ref=view, send_sem=sq_send.at[0], recv_sem=sq_recv.at[slot],
+                device_id=lo_partner, device_id_type=MESH,
+            ).wait_recv()
+        inverse[lax.rem(z, 2), c] = lax.rsqrt(jnp.sum(squares[...], axis=0) / D + 1e-05)
+
+    def inverse_copy(low, core, way, target):
+        view = inverse.at[low, core]
+        return pltpu.make_async_remote_copy(
+            src_ref=view, dst_ref=view, send_sem=inv_send.at[low, way], recv_sem=inv_recv.at[low, core],
+            device_id=target, device_id_type=MESH,
+        )
+
+    def inverse_onward(wanted, low):
+        targets = (above, below, sibling, hi_partner)
+        return [(want, inverse_copy(low, c, way, target)) for way, (want, target) in enumerate(zip(wanted, targets))]
+
     def weights_arrived(part):
-        view = weights.at[1 - yl, pl.ds(part * HALF, HALF)]
-        pltpu.make_async_remote_copy(
-            src_ref=view, dst_ref=view, send_sem=w_send.at[part], recv_sem=w_recv.at[part],
-            device_id=lo_partner, device_id_type=MESH,
-        ).wait_recv()
+        for i, (start, rows, _) in enumerate(PIECES):
+            if start // HALF == part:
+                view = weights.at[1 - yl, pl.ds(start, rows)]
+                pltpu.make_async_remote_copy(
+                    src_ref=view, dst_ref=view, send_sem=w_send.at[i], recv_sem=w_recv.at[i],
+                    device_id=lo_partner, device_id_type=MESH,
+                ).wait_recv()
 
     for load in loads[2:4]:
         load.wait()
@@ -313,34 +387,33 @@
         bias = jnp.where(visible, 0.0, -1e30)
         bias = jnp.concatenate([bias, bias], axis=1)
 
-        def pair(i, _):
-            scores = lax.dot_general(
+        scores = [
+            lax.dot_general(
                 keys_values[j, 0], by_head[i], (((1,), (1,)), ((), ())),
                 preferred_element_type=jnp.float32,
-            ) * HD ** (-0.5)
-            scores = jnp.where(bias < 0.0, -1e30, scores)
-            old = running_max[i]
-            new = jnp.maximum(old, jnp.max(scores, axis=0, keepdims=True))
-            factor = jnp.exp(old - new)
-            parts = jnp.exp(scores - new)
-            running_max[i] = new
+            ) * HD ** (-0.5) + bias
+            for i in range(4)
+        ]
+        olds = [running_max[i] for i in range(4)]
+        news = [jnp.maximum(olds[i], jnp.max(scores[i], axis=0, keepdims=True)) for i in range(4)]
+        for i in range(4):
+            factor = jnp.exp(olds[i] - news[i])
+            parts = jnp.exp(scores[i] - news[i])
+            running_max[i] = news[i]
             denominator[i] = denominator[i] * factor + jnp.sum(parts, axis=0, keepdims=True)
             weighted[i] = weighted[i] * factor + lax.dot_general(
                 keys_values[j, 1], parts.astype(jnp.bfloat16), (((0,), (0,)), ((), ())),
                 preferred_element_type=jnp.float32,
             )
-            return 0
-
-        lax.fori_loop(0, 4, pair, 0)
 
     def attend_step(j, _):
         @pl.when(jnp.logical_and(j < 4, chip > j))
         def _():
             kv_arrival(j + 1, c).wait_recv()
 
-            @pl.when(jnp.logical_and(j < 2, chip < 14))
+            @pl.when(jnp.logical_and(j == 1, kv_sent(3)))
             def _():
-                kv_onward(j + 2, j + 1, 2, after_two).start()
+                kv_onward(3).start()
 
             kv_sibling(j + 1).start()
 
@@ -366,40 +439,21 @@
         residual_ref[:, columns] = rounded
         wide = rounded.astype(jnp.float32)
         total = total + wide * wide
-    squares[mp] = jnp.broadcast_to(jnp.sum(total.T, axis=0, keepdims=True), (8, ROWS))
-
-    def square_copy(peer, i):
-        view = squares.at[mp]
-        return pltpu.make_async_remote_copy(
-            src_ref=view, dst_ref=view, send_sem=sq_send.at[i], recv_sem=sq_recv.at[mp],
-            device_id=peer, device_id_type=MESH,
-        )
-
-    mp_peers = [lo_partner] + x_peers + across
-    for i, peer in enumerate(mp_peers):
-        square_copy(peer, i).start()
-    for i in range(1, 8):
-        slot = lax.rem(mp + i, 8)
-        view = squares.at[slot]
-        pltpu.make_async_remote_copy(
-            src_ref=view, dst_ref=view, send_sem=sq_send.at[0], recv_sem=sq_recv.at[slot],
-            device_id=lo_partner, device_id_type=MESH,
-        ).wait_recv()
-    mean = jnp.sum(squares[...], axis=0) / D
-    inverse = jnp.broadcast_to(lax.rsqrt(mean + 1e-05)[0:1], (ROWS, ROWS)).T
-    for head in range(8):
-        columns = slice(head * HD, (head + 1) * HD)
-        normed_ref[:, columns] = (
-            residual_ref[:, columns].astype(jnp.float32) * inverse * gain_ref[columns].astype(jnp.float32)[None, :]
-        ).astype(jnp.bfloat16)
+        scaled[:, columns] = (wide * gain_ref[columns].astype(jnp.float32)[None, :]).astype(jnp.bfloat16)
 
     @pl.when(match)
     def _():
-        tokens[yh, my_source, yl, mine] = normed_ref[...]
+        tokens[yh, my_source, yl, mine] = scaled[...]
 
     @pl.when(jnp.logical_not(match))
     def _():
         cross_copy().start()
+
+    squares[mp] = jnp.broadcast_to(jnp.sum(total.T, axis=0, keepdims=True), (8, ROWS))
+
+    @pl.when(mp != owner_mp)
+    def _():
+        square_copy().start()
 
     def handle_until(step):
         def one(event, _):
@@ -408,47 +462,57 @@
 
         lax.fori_loop(pick(step, (0,) + BEFORE[:-1]), pick(step, BEFORE), one, 0)
 
-    def first(step, _):
+    def step_through(step, _):
         handle_until(step)
-
-        @pl.when(step == 0)
-        def _():
-            weight_copy(1).start()
+        for i, (_, _, when) in enumerate(PIECES):
+            if when >= 0:
+                @pl.when(step == when)
+                def _():
+                    weight_copy(i).start()
+
+        def each(counts, work):
+            def one(group, _):
+                work(group)
+                return 0
+
+            lax.fori_loop(pick(step, (0,) + counts[:-1]), pick(step, counts), one, 0)
+
+        def gate_group(group):
+            sibling_arrived(group)
+            multiply(group, 0)
+
+        @pl.when(step == 2)
+        def _():
             weights_arrived(0)
 
-        sibling_arrived(step)
-        multiply(step, 0)
+        each(GATED, gate_group)
+
+        @pl.when(step == 3)
+        def _():
+            weights_arrived(1)
+
+        each(UPPED, lambda group: multiply(group, 1))
+
+        def relay_group(group):
+            for part in range(2):
+                add_relayed(group, part)
+
+        each(RELAYED, relay_group)
         return 0
 
-    lax.fori_loop(0, FIRST, first, 0)
-    weights_arrived(1)
-
-    def catch_up(step, _):
-        multiply(step, 1)
-        return 0
-
-    lax.fori_loop(0, FIRST, catch_up, 0)
-
-    def second(step, _):
-        handle_until(step)
-        sibling_arrived(step)
-        for part in range(2):
-            multiply(step, part)
-        for part in range(2):
-            add_relayed(step - FIRST, part)
-        return 0
-
-    lax.fori_loop(FIRST, 8, second, 0)
+    lax.fori_loop(0, 8, step_through, 0)
 
     def last(step, _):
         for part in range(2):
             add_relayed(step, part)
         return 0
 
-    lax.fori_loop(8 - FIRST, 8, last, 0)
+    lax.fori_loop(RELAYED[-1], 8, last, 0)
 
     for low in range(2):
         totals = []
+        inverse_copy(low, 1 - c, 0, sibling).wait_recv()
+        scale = jnp.concatenate([inverse[low, 0], inverse[low, 1]], axis=1)[0:1]
         for part in range(2):
             rows = pl.ds(part * HALF, HALF)
             total = own_sum[low, rows]
@@ -459,22 +523,25 @@
                     recv_sem=sum_recv.at[slot, low, part], device_id=x_peers[0], device_id_type=MESH,
                 ).wait_recv()
                 total = total + landed[slot, low, rows].astype(jnp.float32)
-            totals.append(total)
+            totals.append(total * scale)
         gate, up = totals
         out_ref[:, low * 256:(low + 1) * 256] = (gate / (1.0 + jnp.exp(-gate)) * up).astype(jnp.bfloat16)
 
-    for i, j, ahead, target in ((0, 0, 1, after), (1, 0, 2, after_two), (2, 1, 2, after_two), (3, 2, 2, after_two)):
-        @pl.when(jnp.logical_and(chip < 16 - ahead, chip >= j))
-        def _():
-            kv_onward(i, j, ahead, target).wait_send()
+    for i in range(4):
+        @pl.when(kv_sent(i))
+        def _():
+            kv_onward(i).wait_send()
     for j in range(5):
         @pl.when(chip >= j)
         def _():
             kv_sibling(j).wait_send()
-    for i, peer in enumerate(mp_peers):
-        square_copy(peer, i).wait_send()
-    for part in range(2):
-        weight_copy(part).wait_send()
+
+    @pl.when(mp != owner_mp)
+    def _():
+        square_copy().wait_send()
+
+    for i in range(len(PIECES)):
+        weight_copy(i).wait_send()
 
     @pl.when(jnp.logical_not(match))
     def _():
@@ -485,6 +552,13 @@
         h, source, _ = unit_of(unit, half)
         for kb in range(2):
             for wanted, copy in onward(unit, half, kb):
+                @pl.when(wanted)
+                def _():
+                    copy.wait_send()
+
+        @pl.when(owned_here(h, source))
+        def _():
+            for wanted, copy in inverse_onward(ways_on(unit, half), lax.rem(source, 2)):
                 @pl.when(wanted)
                 def _():
                     copy.wait_send()
@@ -530,11 +604,12 @@
             pltpu.VMEM((ROWS, KB), jnp.bfloat16),
             pltpu.VMEM((ROWS, KB), jnp.bfloat16),
             pltpu.VMEM((8, 8, ROWS), jnp.float32),
+            pltpu.VMEM((2, 2, 8, ROWS), jnp.float32),
             pltpu.VMEM((4, 1, 2 * ROWS), jnp.float32),
             pltpu.VMEM((4, 1, 2 * ROWS), jnp.float32),
             pltpu.VMEM((4, HD, 2 * ROWS), jnp.float32),
-            dma((6,)), dma((4,)), dma((5,)), dma((5, 2)), dma((7,)), dma((8,)),
-            dma((2,)), dma((2,)), dma((1,)), dma((2, 4, 2, 2)),
+            dma((6,)), dma((4,)), dma((5,)), dma((5, 2)), dma((1,)), dma((8,)), dma((2, 4)), dma((2, 2)),
+            dma((3,)), dma((3,)), dma((1,)), dma((2, 4, 2, 2)),
             dma((2, 4, 2)), dma((2, 4, 2)), dma((2, 4, 2)), dma((2, 4, 2)),
             dma((2, 4, 2)), dma((2, 4)), dma((2, 4, 2)), dma((2, 2, 2)),
         ],

time: 115 us -> 110 us (0.957)
  Pallas kernels: 110 us -> 106 us
    pallas_call x1, Pallas kernels: 110 us -> 106 us  [on_device(): pl.pallas_call(layer_kernel, out_shape=(jax.ShapeDtypeStruct((ROWS, KB),...]
where the time goes in v5:
time: 110 us; the launch traced here: 109 us
  Pallas kernels  106 us (96%)
  local copies, waits for them, and re-layouts  2.49 us (2%)
    pallas_call x1, Pallas kernels, on_device(): pl.pallas_call(layer_kernel, out_shape=(jax.ShapeDtypeStruct((ROWS, KB),...  106 us
    unnamed x4, local copies, waits for them, and re-layouts  2.49 us

profile of v5, /device:TPU:25, one launch (start us, length us, event | category | flops | bytes accessed | tf_op | source)
XLA Modules:
  0.0 108.7 jit_solution(89700059866260767)
XLA Ops:
  0.6 105.5 %layer.1 = (bf16[128,1024]{1,0:T(8,128)(2,1)}, bf16[448,512]{1,0:T(8,128)(2,1)}) custom-call(s32[16]{0:T(128)} %lengths_ref.1, bf16[128,1024]{1,0:T(8,128)(2,1)} %query_ref.1, bf16[128,128]{1,0:T(8,128)(2,1)} %key_ref.1, bf16[128,128]{1,0:T(8,128)(2,1)} %value_ref.1, bf16[128,1024]{1,0:T(8,128)(2,1)} %residual_in_ref.1, bf16[1024]{0:T(1024)(128)(2,1)} %gain_ref.1, ...), custom_call_target="tpu_custom_call" | custom-call | tf_op jit(solution)/shard_map/layer/pallas_call | solution.py:586
  106.2 0.0 copy-start
  106.2 1.7 %copy.12 = bf16[128,1024]{1,0:T(8,128)(2,1)} copy(bf16[128,1024]{1,0:T(8,128)(2,1)} %get-tuple-element.8) | data formatting | bytes 524288
  107.9 0.0 copy-done
  107.9 0.8 copy.13
Async XLA Ops:
  106.2 1.7 %copy-start = (bf16[448,512]{1,0:T(8,128)(2,1)S(1)}, bf16[448,512]{1,0:T(8,128)(2,1)}, u32[]{:S(2)}) copy-start(bf16[448,512]{1,0:T(8,128)(2,1)} %get-tuple-element.5) | copy-start | bytes 1376260

commit v6 on v5

--- a/solution.py
+++ b/solution.py
@@ -14,6 +14,7 @@
 KB = 1024
 HALF = 448
 WIDTH = 2 * HALF
+QUARTER = HALF // 2
 
 
 def place():
@@ -267,21 +268,22 @@
     def goes_up(source, part):
         return lax.rem(source + part, 2) == 0
 
-    def sum_copy(h, source, part):
-        rows = pl.ds(part * HALF, HALF)
+    def sum_copy(h, source, quarter):
+        rows = pl.ds(quarter * QUARTER, QUARTER)
         slot = role_of(h, source) // 2
         low = lax.rem(source, 2)
         return pltpu.make_async_remote_copy(
             src_ref=staged.at[h, source, rows], dst_ref=landed.at[slot, low, rows],
-            send_sem=sum_send.at[h, source, part], recv_sem=sum_recv.at[slot, low, part],
+            send_sem=sum_send.at[h, source, quarter], recv_sem=sum_recv.at[slot, low, quarter],
             device_id=device(yh, z, c, h * 2 + source // 2, yl), device_id_type=MESH,
         )
 
-    def relay_copy(h, source, part):
-        towards = lax.rem(x + jnp.where(goes_up(source, part), 1, 3), 4)
-        return pltpu.make_async_remote_copy(
-            src_ref=staged.at[h, source, pl.ds(part * HALF, HALF)], dst_ref=relayed.at[h, source],
-            send_sem=relay_send.at[h, source, part], recv_sem=relay_recv.at[h, source],
+    def relay_copy(h, source, quarter):
+        towards = lax.rem(x + jnp.where(goes_up(source, quarter // 2), 1, 3), 4)
+        return pltpu.make_async_remote_copy(
+            src_ref=staged.at[h, source, pl.ds(quarter * QUARTER, QUARTER)],
+            dst_ref=relayed.at[h, source, quarter % 2],
+            send_sem=relay_send.at[h, source, quarter], recv_sem=relay_recv.at[h, source, quarter % 2],
             device_id=device(yh, z, c, towards, yl), device_id_type=MESH,
         )
 
@@ -309,23 +311,27 @@
 
         @pl.when(role == 2)
         def _():
-            relay_copy(h, source, part).start()
+            for quarter in (2 * part, 2 * part + 1):
+                relay_copy(h, source, quarter).start()
 
         @pl.when(jnp.logical_and(lax.rem(role, 2) == 1, jnp.logical_not(relays(role, source, part))))
         def _():
-            sum_copy(h, source, part).start()
+            for quarter in (2 * part, 2 * part + 1):
+                sum_copy(h, source, quarter).start()
 
     def add_relayed(step, part):
         h, source = group_of(step)
-        rows = pl.ds(part * HALF, HALF)
 
         @pl.when(relays(role_of(h, source), source, part))
         def _():
-            relay_copy(h, source, part).wait_recv()
-            staged[h, source, rows] = (
-                staged[h, source, rows].astype(jnp.float32) + relayed[h, source].astype(jnp.float32)
-            ).astype(jnp.bfloat16)
-            sum_copy(h, source, part).start()
+            for quarter in (2 * part, 2 * part + 1):
+                rows = pl.ds(quarter * QUARTER, QUARTER)
+                relay_copy(h, source, quarter).wait_recv()
+                staged[h, source, rows] = (
+                    staged[h, source, rows].astype(jnp.float32)
+                    + relayed[h, source, quarter % 2].astype(jnp.float32)
+                ).astype(jnp.bfloat16)
+                sum_copy(h, source, quarter).start()
 
     def sibling_arrived(step):
         h, source = group_of(step)
@@ -510,22 +516,25 @@
     lax.fori_loop(RELAYED[-1], 8, last, 0)
 
     for low in range(2):
-        totals = []
         inverse_copy(low, 1 - c, 0, sibling).wait_recv()
         scale = jnp.concatenate([inverse[low, 0], inverse[low, 1]], axis=1)[0:1]
-        for part in range(2):
-            rows = pl.ds(part * HALF, HALF)
+        def total_of(quarter):
+            rows = pl.ds(quarter * QUARTER, QUARTER)
             total = own_sum[low, rows]
             for slot in range(2):
                 view = landed.at[slot, low, rows]
                 pltpu.make_async_remote_copy(
-                    src_ref=view, dst_ref=view, send_sem=sum_send.at[0, 0, part],
-                    recv_sem=sum_recv.at[slot, low, part], device_id=x_peers[0], device_id_type=MESH,
+                    src_ref=view, dst_ref=view, send_sem=sum_send.at[0, 0, quarter],
+                    recv_sem=sum_recv.at[slot, low, quarter], device_id=x_peers[0], device_id_type=MESH,
                 ).wait_recv()
                 total = total + landed[slot, low, rows].astype(jnp.float32)
-            totals.append(total * scale)
-        gate, up = totals
-        out_ref[:, low * 256:(low + 1) * 256] = (gate / (1.0 + jnp.exp(-gate)) * up).astype(jnp.bfloat16)
+            return total * scale
+
+        for i in range(2):
+            gate, up = total_of(i), total_of(2 + i)
+            out_ref[i * QUARTER:(i + 1) * QUARTER, low * 256:(low + 1) * 256] = (
+                gate / (1.0 + jnp.exp(-gate)) * up
+            ).astype(jnp.bfloat16)
 
     for i in range(4):
         @pl.when(kv_sent(i))
@@ -564,17 +573,28 @@
                     copy.wait_send()
 
         role = role_of(h, source)
-        for part in range(2):
+        for quarter in range(4):
             @pl.when(role == 2)
             def _():
-                relay_copy(h, source, part).wait_send()
+                relay_copy(h, source, quarter).wait_send()
 
             @pl.when(lax.rem(role, 2) == 1)
             def _():
-                sum_copy(h, source, part).wait_send()
+                sum_copy(h, source, quarter).wait_send()
         return 0
 
     lax.fori_loop(0, 8, drain, 0)
+
+
+def hand_over_kernel(residual_ref, hidden_ref, residual_out, hidden_out, sems):
+    copies = (
+        pltpu.make_async_copy(residual_ref, residual_out, sems.at[0]),
+        pltpu.make_async_copy(hidden_ref, hidden_out, sems.at[1]),
+    )
+    for copy in copies:
+        copy.start()
+    for copy in copies:
+        copy.wait()
 
 
 def on_device(
@@ -595,7 +615,7 @@
             pltpu.VMEM((2, 4, 2, 2 * ROWS, KB), jnp.bfloat16),
             pltpu.VMEM((2, WIDTH, KB), jnp.bfloat16),
             pltpu.VMEM((2, 4, WIDTH, 2 * ROWS), jnp.bfloat16),
-            pltpu.VMEM((2, 4, HALF, 2 * ROWS), jnp.bfloat16),
+            pltpu.VMEM((2, 4, 2, QUARTER, 2 * ROWS), jnp.bfloat16),
             pltpu.VMEM((2, 2, WIDTH, 2 * ROWS), jnp.bfloat16),
             pltpu.VMEM((2, WIDTH, 2 * ROWS), jnp.float32),
             pltpu.VMEM((ROWS, KB), jnp.bfloat16),
@@ -611,7 +631,7 @@
             dma((6,)), dma((4,)), dma((5,)), dma((5, 2)), dma((1,)), dma((8,)), dma((2, 4)), dma((2, 2)),
             dma((3,)), dma((3,)), dma((1,)), dma((2, 4, 2, 2)),
             dma((2, 4, 2)), dma((2, 4, 2)), dma((2, 4, 2)), dma((2, 4, 2)),
-            dma((2, 4, 2)), dma((2, 4)), dma((2, 4, 2)), dma((2, 2, 2)),
+            dma((2, 4, 4)), dma((2, 4, 2)), dma((2, 4, 4)), dma((2, 2, 4)),
         ],
         compiler_params=pltpu.CompilerParams(
             collective_id=0, has_side_effects=True, vmem_limit_bytes=56 * 2**20
@@ -621,6 +641,17 @@
         doc_lengths, query_heads, key_heads, value_heads, residual_in,
         norm_gain, gate_weight.T, up_weight.T,
     )
+    residual, hidden = pl.pallas_call(
+        hand_over_kernel,
+        out_shape=(
+            jax.ShapeDtypeStruct((ROWS, KB), jnp.bfloat16),
+            jax.ShapeDtypeStruct((HALF, 4 * ROWS), jnp.bfloat16),
+        ),
+        in_specs=[anywhere] * 2,
+        out_specs=(anywhere, anywhere),
+        scratch_shapes=[dma((2,))],
+        name="hand_over",
+    )(residual, hidden)
     return residual, hidden.T
 
 

time: 110 us -> 129 us (1.17)
  Pallas kernels: 106 us -> 127 us
  local copies, waits for them, and re-layouts: 2.49 us -> 0 us
    pallas_call x0 -> x1, Pallas kernels: none -> 23 us  [on_device(): pl.pallas_call(hand_over_kernel, out_shape=(jax.ShapeDtypeStruct((ROWS, K...]
    unnamed x4 -> x0, local copies, waits for them, and re-layouts: 2.49 us -> none
where the time goes in v6:
time: 129 us; the launch traced here: 128 us
  Pallas kernels  127 us (98%)
    pallas_call x1, Pallas kernels, on_device(): pl.pallas_call(layer_kernel, out_shape=(jax.ShapeDtypeStruct((ROWS, KB),...  105 us
    pallas_call x1, Pallas kernels, on_device(): pl.pallas_call(hand_over_kernel, out_shape=(jax.ShapeDtypeStruct((ROWS, K...  23 us

profile of v6, /device:TPU:25, one launch (start us, length us, event | category | flops | bytes accessed | tf_op | source)
XLA Modules:
  0.0 128.1 jit_solution(16545257665308603485)
XLA Ops:
  0.6 104.5 %layer.1 = (bf16[128,1024]{1,0:T(8,128)(2,1)}, bf16[448,512]{1,0:T(8,128)(2,1)}) custom-call(s32[16]{0:T(128)} %lengths_ref.1, bf16[128,1024]{1,0:T(8,128)(2,1)} %query_ref.1, bf16[128,128]{1,0:T(8,128)(2,1)} %key_ref.1, bf16[128,128]{1,0:T(8,128)(2,1)} %value_ref.1, bf16[128,1024]{1,0:T(8,128)(2,1)} %residual_in_ref.1, bf16[1024]{0:T(1024)(128)(2,1)} %gain_ref.1, ...), custom_call_target="tpu_custom_call" | custom-call | tf_op jit(solution)/shard_map/layer/pallas_call | solution.py:606
  105.1 23.0 %hand_over.1 = (bf16[128,1024]{1,0:T(8,128)(2,1)}, bf16[448,512]{1,0:T(8,128)(2,1)}) custom-call(bf16[128,1024]{1,0:T(8,128)(2,1)} %get-tuple-element.6.residual_ref, bf16[448,512]{1,0:T(8,128)(2,1)} %get-tuple-element.7.hidden_ref), custom_call_target="tpu_custom_call" | custom-call | tf_op jit(solution)/shard_map/hand_over/pallas_call | solution.py:644

commit v7 on v6

--- a/solution.py
+++ b/solution.py
@@ -196,50 +196,58 @@
             recv_sem=tok_recv.at[h, source, kb, core], device_id=sibling, device_id_type=MESH,
         )
 
-    def by_place(step, tables):
-        codes = [[u * 4 + sum(b << i for i, b in enumerate(rest)) for u, *rest in t] for t in tables]
-        code = jnp.where(w < 2, pick(step, codes[0]), pick(step, codes[1]))
-        return code // 4, lax.rem(code, 2), lax.rem(code // 2, 2)
-
-    def unit_of(unit, half):
-        table = lambda rows: pick(unit * 4 + w, [v for row in rows for v in row])
-        source_z = lax.rem(z + table(OFFSETS) + 8, 8)
+    def event_code(event, v):
+        unit, half, block = EVENTS[v // 2][event]
+        bits = (
+            half, block, ONWARD_UP[half][unit][v], ONWARD_DOWN[half][unit][v],
+            CROSSES[unit][v] * (1 - half), int(unit == 0 and v < 2 and half == 0),
+        )
+        return OFFSETS[unit][v] + 4 + sum(b << (4 + i) for i, b in enumerate(bits))
+
+    def group_code(step, v):
+        unit, half = GROUPS[v // 2][step]
+        return OFFSETS[unit][v] + 4 + (half << 4)
+
+    event_codes = [pick(w, [event_code(e, v) for v in range(4)]) for e in range(16)]
+    group_codes = [pick(w, [group_code(g, v) for v in range(4)]) for g in range(8)]
+
+    def bit(code, i):
+        return lax.rem(code // 2**i, 2)
+
+    def unit_of(code):
+        source_z = lax.rem(z + lax.rem(code, 16) + 4, 8)
         source = (source_z // 4) * 2 + lax.rem(source_z, 2)
-        return lax.rem(yh + half, 2), source, table
+        return lax.rem(yh + bit(code, 4), 2), source
 
     def group_of(step):
-        unit, half, _ = by_place(step, GROUPS)
-        h, source, _ = unit_of(unit, half)
-        return h, source
-
-    def ways_on(unit, half):
-        _, _, table = unit_of(unit, half)
-        by_half = lambda tables: jnp.where(half == 0, table(tables[0]), table(tables[1])) == 1
-        crosses = jnp.logical_and(table(CROSSES) == 1, half == 0)
-        return by_half(ONWARD_UP), by_half(ONWARD_DOWN), unit >= 0, crosses
-
-    def onward(unit, half, kb):
-        h, source, _ = unit_of(unit, half)
+        return unit_of(pick(step, group_codes))
+
+    def event_of(event):
+        code = pick(event, event_codes)
+        h, source = unit_of(code)
+        block = bit(code, 5)
+        goes = (bit(code, 6) == 1, bit(code, 7) == 1, block >= 0, bit(code, 8) == 1)
+        return h, source, block, goes, bit(code, 9) == 1
+
+    def onward(h, source, kb, goes):
         ways = ((up_send, above), (down_send, below), (sib_send, sibling), (hi_send, hi_partner))
         return [
             (wanted, token_copy(h, source, kb, sems, target))
-            for wanted, (sems, target) in zip(ways_on(unit, half), ways)
+            for wanted, (sems, target) in zip(goes, ways)
         ]
 
     def owned_here(h, source):
         return h * 2 + source // 2 == x
 
     def handle(event):
-        unit, half, block = by_place(event, EVENTS)
-        h, source, _ = unit_of(unit, half)
+        h, source, block, goes, at_home = event_of(event)
         kb = lax.rem(yl + block, 2)
-        own = jnp.logical_and(match, unit == 0)
-
-        @pl.when(jnp.logical_not(jnp.logical_and(own, jnp.logical_and(half == 0, block == 0))))
+
+        @pl.when(jnp.logical_not(jnp.logical_and(at_home, block == 0)))
         def _():
             token_arrival(h, source, kb, c).wait_recv()
 
-        for wanted, copy in onward(unit, half, kb):
+        for wanted, copy in onward(h, source, kb, goes):
             @pl.when(wanted)
             def _():
                 copy.start()
@@ -247,7 +255,6 @@
         @pl.when(jnp.logical_and(owned_here(h, source), block == 1))
         def _():
             low = lax.rem(source, 2)
-            at_home = jnp.logical_and(own, half == 0)
 
             @pl.when(at_home)
             def _():
@@ -257,7 +264,7 @@
             def _():
                 inverse_copy(low, c, 0, sibling).wait_recv()
 
-            for wanted, copy in inverse_onward(ways_on(unit, half), low):
+            for wanted, copy in inverse_onward(goes, low):
                 @pl.when(wanted)
                 def _():
                     copy.start()
@@ -515,6 +522,44 @@
 
     lax.fori_loop(RELAYED[-1], 8, last, 0)
 
+    for i in range(4):
+        @pl.when(kv_sent(i))
+        def _():
+            kv_onward(i).wait_send()
+    for j in range(5):
+        @pl.when(chip >= j)
+        def _():
+            kv_sibling(j).wait_send()
+
+    @pl.when(mp != owner_mp)
+    def _():
+        square_copy().wait_send()
+
+    for i in range(len(PIECES)):
+        weight_copy(i).wait_send()
+
+    @pl.when(jnp.logical_not(match))
+    def _():
+        cross_copy().wait_send()
+
+    def tokens_sent(event, _):
+        h, source, block, goes, _ = event_of(event)
+        for wanted, copy in onward(h, source, lax.rem(yl + block, 2), goes):
+            @pl.when(wanted)
+            def _():
+                copy.wait_send()
+
+        @pl.when(jnp.logical_and(owned_here(h, source), block == 1))
+        def _():
+            for wanted, copy in inverse_onward(goes, lax.rem(source, 2)):
+                @pl.when(wanted)
+                def _():
+                    copy.wait_send()
+
+        return 0
+
+    lax.fori_loop(0, 16, tokens_sent, 0)
+
     for low in range(2):
         inverse_copy(low, 1 - c, 0, sibling).wait_recv()
         scale = jnp.concatenate([inverse[low, 0], inverse[low, 1]], axis=1)[0:1]
@@ -530,48 +575,11 @@
                 total = total + landed[slot, low, rows].astype(jnp.float32)
             return total * scale
 
-        for i in range(2):
-            gate, up = total_of(i), total_of(2 + i)
-            out_ref[i * QUARTER:(i + 1) * QUARTER, low * 256:(low + 1) * 256] = (
-                gate / (1.0 + jnp.exp(-gate)) * up
-            ).astype(jnp.bfloat16)
-
-    for i in range(4):
-        @pl.when(kv_sent(i))
-        def _():
-            kv_onward(i).wait_send()
-    for j in range(5):
-        @pl.when(chip >= j)
-        def _():
-            kv_sibling(j).wait_send()
-
-    @pl.when(mp != owner_mp)
-    def _():
-        square_copy().wait_send()
-
-    for i in range(len(PIECES)):
-        weight_copy(i).wait_send()
-
-    @pl.when(jnp.logical_not(match))
-    def _():
-        cross_copy().wait_send()
-
-    def drain(step, _):
-        unit, half = step // 2, lax.rem(step, 2)
-        h, source, _ = unit_of(unit, half)
-        for kb in range(2):
-            for wanted, copy in onward(unit, half, kb):
-                @pl.when(wanted)
-                def _():
-                    copy.wait_send()
-
-        @pl.when(owned_here(h, source))
-        def _():
-            for wanted, copy in inverse_onward(ways_on(unit, half), lax.rem(source, 2)):
-                @pl.when(wanted)
-                def _():
-                    copy.wait_send()
-
+        for quarter in range(4):
+            out_ref[quarter * QUARTER:(quarter + 1) * QUARTER, low * 256:(low + 1) * 256] = total_of(quarter)
+
+    def sums_sent(step, _):
+        h, source = group_of(step)
         role = role_of(h, source)
         for quarter in range(4):
             @pl.when(role == 2)
@@ -581,20 +589,10 @@
             @pl.when(lax.rem(role, 2) == 1)
             def _():
                 sum_copy(h, source, quarter).wait_send()
+
         return 0
 
-    lax.fori_loop(0, 8, drain, 0)
-
-
-def hand_over_kernel(residual_ref, hidden_ref, residual_out, hidden_out, sems):
-    copies = (
-        pltpu.make_async_copy(residual_ref, residual_out, sems.at[0]),
-        pltpu.make_async_copy(hidden_ref, hidden_out, sems.at[1]),
-    )
-    for copy in copies:
-        copy.start()
-    for copy in copies:
-        copy.wait()
+    lax.fori_loop(0, 8, sums_sent, 0)
 
 
 def on_device(
@@ -603,11 +601,11 @@
     dma = pltpu.SemaphoreType.DMA
     vmem = pl.BlockSpec(memory_space=pltpu.VMEM)
     anywhere = pl.BlockSpec(memory_space=pl.ANY)
-    residual, hidden = pl.pallas_call(
+    residual, sums = pl.pallas_call(
         layer_kernel,
         out_shape=(
             jax.ShapeDtypeStruct((ROWS, KB), jnp.bfloat16),
-            jax.ShapeDtypeStruct((HALF, 4 * ROWS), jnp.bfloat16),
+            jax.ShapeDtypeStruct((WIDTH, 4 * ROWS), jnp.float32),
         ),
         in_specs=[pl.BlockSpec(memory_space=pltpu.SMEM)] + [anywhere] * 4 + [vmem] + [anywhere] * 2,
         out_specs=(vmem, vmem),
@@ -641,17 +639,8 @@
         doc_lengths, query_heads, key_heads, value_heads, residual_in,
         norm_gain, gate_weight.T, up_weight.T,
     )
-    residual, hidden = pl.pallas_call(
-        hand_over_kernel,
-        out_shape=(
-            jax.ShapeDtypeStruct((ROWS, KB), jnp.bfloat16),
-            jax.ShapeDtypeStruct((HALF, 4 * ROWS), jnp.bfloat16),
-        ),
-        in_specs=[anywhere] * 2,
-        out_specs=(anywhere, anywhere),
-        scratch_shapes=[dma((2,))],
-        name="hand_over",
-    )(residual, hidden)
+    gate, up = sums[:HALF], sums[HALF:]
+    hidden = (jax.nn.silu(gate) * up).astype(jnp.bfloat16)
     return residual, hidden.T
 
 

time: 129 us -> 110 us (0.85)
  Pallas kernels: 127 us -> 105 us
  other arithmetic: 0 us -> 2.54 us
    pallas_call x1 -> x0, Pallas kernels: 23 us -> none  [on_device(): pl.pallas_call(hand_over_kernel, out_shape=(jax.ShapeDtypeStruct((ROWS, K...]
    transpose x0 -> x1, other arithmetic: none -> 2.54 us  [on_device(): return (residual, hidden.T)]
where the time goes in v7:
time: 110 us; the launch traced here: 109 us
  Pallas kernels  105 us (95%)
  other arithmetic  2.54 us (2%)
    pallas_call x1, Pallas kernels, on_device(): pl.pallas_call(layer_kernel, out_shape=(jax.ShapeDtypeStruct((ROWS, KB),...  105 us
    transpose x1, other arithmetic, on_device(): return (residual, hidden.T)  2.54 us

profile of v7, /device:TPU:25, one launch (start us, length us, event | category | flops | bytes accessed | tf_op | source)
XLA Modules:
  0.0 108.6 jit_solution(9411448797672059398)
XLA Ops:
  0.6 104.7 %layer.1 = (bf16[128,1024]{1,0:T(8,128)(2,1)}, f32[896,512]{1,0:T(8,128)}) custom-call(s32[16]{0:T(128)} %lengths_ref.1, bf16[128,1024]{1,0:T(8,128)(2,1)} %query_ref.1, bf16[128,128]{1,0:T(8,128)(2,1)} %key_ref.1, bf16[128,128]{1,0:T(8,128)(2,1)} %value_ref.1, bf16[128,1024]{1,0:T(8,128)(2,1)} %residual_in_ref.1, bf16[1024]{0:T(1024)(128)(2,1)} %gain_ref.1, ...), custom_call_target="tpu_custom_call" | custom-call | tf_op jit(solution)/shard_map/layer/pallas_call | solution.py:604
  105.4 0.0 copy-start
  105.4 2.5 %fusion = bf16[512,448]{0,1:T(8,128)(2,1)} fusion(f32[896,512]{1,0:T(8,128)} %get-tuple-element.5), kind=kLoop, calls=%fused_computation.1 | loop fusion | flops 1376256 | bytes 2293760 | tf_op jit(solution)/shard_map/transpose | solution.py:644
  107.9 0.0 copy-done
  107.9 0.7 copy.11
Async XLA Ops:
  105.4 2.5 %copy-start = (bf16[128,1024]{1,0:T(8,128)(2,1)S(1)}, bf16[128,1024]{1,0:T(8,128)(2,1)}, u32[]{:S(2)}) copy-start(bf16[128,1024]{1,0:T(8,128)(2,1)} %get-tuple-element.8) | copy-start | bytes 786436

commit v8 on v7

--- a/solution.py
+++ b/solution.py
@@ -273,7 +273,7 @@
         return lax.rem(x - (h * 2 + source // 2) + 4, 4)
 
     def goes_up(source, part):
-        return lax.rem(source + part, 2) == 0
+        return lax.rem(source + part + c, 2) == 0
 
     def sum_copy(h, source, quarter):
         rows = pl.ds(quarter * QUARTER, QUARTER)
@@ -575,8 +575,11 @@
                 total = total + landed[slot, low, rows].astype(jnp.float32)
             return total * scale
 
-        for quarter in range(4):
-            out_ref[quarter * QUARTER:(quarter + 1) * QUARTER, low * 256:(low + 1) * 256] = total_of(quarter)
+        for i in range(2):
+            gate, up = total_of(i), total_of(2 + i)
+            out_ref[i * QUARTER:(i + 1) * QUARTER, low * 256:(low + 1) * 256] = (
+                gate / (1.0 + jnp.exp(-gate)) * up
+            ).astype(jnp.bfloat16)
 
     def sums_sent(step, _):
         h, source = group_of(step)
@@ -601,11 +604,11 @@
     dma = pltpu.SemaphoreType.DMA
     vmem = pl.BlockSpec(memory_space=pltpu.VMEM)
     anywhere = pl.BlockSpec(memory_space=pl.ANY)
-    residual, sums = pl.pallas_call(
+    residual, hidden = pl.pallas_call(
         layer_kernel,
         out_shape=(
             jax.ShapeDtypeStruct((ROWS, KB), jnp.bfloat16),
-            jax.ShapeDtypeStruct((WIDTH, 4 * ROWS), jnp.float32),
+            jax.ShapeDtypeStruct((HALF, 4 * ROWS), jnp.bfloat16),
         ),
         in_specs=[pl.BlockSpec(memory_space=pltpu.SMEM)] + [anywhere] * 4 + [vmem] + [anywhere] * 2,
         out_specs=(vmem, vmem),
@@ -639,8 +642,6 @@
         doc_lengths, query_heads, key_heads, value_heads, residual_in,
         norm_gain, gate_weight.T, up_weight.T,
     )
-    gate, up = sums[:HALF], sums[HALF:]
-    hidden = (jax.nn.silu(gate) * up).astype(jnp.bfloat16)
     return residual, hidden.T
 
 

time: 110 us -> 108 us (0.982)
  other arithmetic: 2.54 us -> 0 us
  local copies, waits for them, and re-layouts: 0.71 us -> 2.49 us
    transpose x1 -> x0, other arithmetic: 2.54 us -> none  [on_device(): return (residual, hidden.T)]
    unnamed x3 -> x4, local copies, waits for them, and re-layouts: 0.71 us -> 2.49 us
where the time goes in v8:
time: 108 us; the launch traced here: 107 us
  Pallas kernels  104 us (96%)
  local copies, waits for them, and re-layouts  2.49 us (2%)
    pallas_call x1, Pallas kernels, on_device(): pl.pallas_call(layer_kernel, out_shape=(jax.ShapeDtypeStruct((ROWS, KB),...  104 us
    unnamed x4, local copies, waits for them, and re-layouts  2.49 us

profile of v8, /device:TPU:25, one launch (start us, length us, event | category | flops | bytes accessed | tf_op | source)
XLA Modules:
  0.0 107.3 jit_solution(16291988556309494027)
XLA Ops:
  0.6 104.2 %layer.1 = (bf16[128,1024]{1,0:T(8,128)(2,1)}, bf16[448,512]{1,0:T(8,128)(2,1)}) custom-call(s32[16]{0:T(128)} %lengths_ref.1, bf16[128,1024]{1,0:T(8,128)(2,1)} %query_ref.1, bf16[128,128]{1,0:T(8,128)(2,1)} %key_ref.1, bf16[128,128]{1,0:T(8,128)(2,1)} %value_ref.1, bf16[128,1024]{1,0:T(8,128)(2,1)} %residual_in_ref.1, bf16[1024]{0:T(1024)(128)(2,1)} %gain_ref.1, ...), custom_call_target="tpu_custom_call" | custom-call | tf_op jit(solution)/shard_map/layer/pallas_call | solution.py:607
  104.8 0.0 copy-start
  104.8 1.7 %copy.12 = bf16[128,1024]{1,0:T(8,128)(2,1)} copy(bf16[128,1024]{1,0:T(8,128)(2,1)} %get-tuple-element.8) | data formatting | bytes 524288
  106.6 0.0 copy-done
  106.6 0.8 copy.13
Async XLA Ops:
  104.8 1.7 %copy-start = (bf16[448,512]{1,0:T(8,128)(2,1)S(1)}, bf16[448,512]{1,0:T(8,128)(2,1)}, u32[]{:S(2)}) copy-start(bf16[448,512]{1,0:T(8,128)(2,1)} %get-tuple-element.5) | copy-start | bytes 1376260

commit v9 on v8

--- a/solution.py
+++ b/solution.py
@@ -92,7 +92,7 @@
     mp = x * 2 + yl
     chip = yh * 8 + z
     step_on = lambda k: device(lax.rem((chip + 16 + k) // 8, 2), lax.rem(chip + 16 + k, 8), c, x, yl)
-    kv_hops = ((0, 1, step_on(1)), (0, 2, step_on(2)), (0, 4, step_on(4)), (2, 1, step_on(1)))
+    kv_hops = ((0, 1, step_on(1)), (0, 2, step_on(2)), (1, 2, step_on(2)), (2, 2, step_on(2)))
 
     loads = [
         pltpu.make_async_copy(key_ref, keys_values.at[0, 0, mine], load_sem.at[0]),
@@ -115,14 +115,13 @@
     def _():
         pl.semaphore_signal(barrier, inc=1, device_id=step_on(-1), device_id_type=MESH)
 
-    for k in (2, 4):
-        @pl.when(chip >= k)
-        def _():
-            pl.semaphore_signal(barrier, inc=1, device_id=step_on(-k), device_id_type=MESH)
+    @pl.when(chip >= 2)
+    def _():
+        pl.semaphore_signal(barrier, inc=1, device_id=step_on(-2), device_id_type=MESH)
 
     pl.semaphore_wait(
         barrier,
-        len(peers) + jnp.where(chip == 7, 1, 0) + jnp.where(chip < 14, 1, 0) + jnp.where(chip < 12, 1, 0),
+        len(peers) + jnp.where(chip == 7, 1, 0) + jnp.where(chip < 14, 1, 0),
     )
     for load in loads[:2]:
         load.wait()
@@ -153,7 +152,7 @@
             device_id=sibling, device_id_type=MESH,
         )
 
-    for i in range(3):
+    for i in range(2):
         @pl.when(kv_sent(i))
         def _():
             kv_onward(i).start()
@@ -424,9 +423,10 @@
         def _():
             kv_arrival(j + 1, c).wait_recv()
 
-            @pl.when(jnp.logical_and(j == 1, kv_sent(3)))
-            def _():
-                kv_onward(3).start()
+            for i in (2, 3):
+                @pl.when(jnp.logical_and(j == i - 2, kv_sent(i)))
+                def _():
+                    kv_onward(i).start()
 
             kv_sibling(j + 1).start()
 

time: 108 us -> 106 us (0.981)
    pallas_call x1, Pallas kernels: 104 us -> 103 us  [on_device(): pl.pallas_call(layer_kernel, out_shape=(jax.ShapeDtypeStruct((ROWS, KB),...]
where the time goes in v9:
time: 106 us
  Pallas kernels  103 us (97%)
  local copies, waits for them, and re-layouts  2.49 us (2%)
    pallas_call x1, Pallas kernels, on_device(): pl.pallas_call(layer_kernel, out_shape=(jax.ShapeDtypeStruct((ROWS, KB),...  103 us
    unnamed x4, local copies, waits for them, and re-layouts  2.49 us

profile of v9, /device:TPU:25, one launch (start us, length us, event | category | flops | bytes accessed | tf_op | source)
XLA Modules:
  0.0 105.9 jit_solution(9963868738829388887)
XLA Ops:
  0.6 102.8 %layer.1 = (bf16[128,1024]{1,0:T(8,128)(2,1)}, bf16[448,512]{1,0:T(8,128)(2,1)}) custom-call(s32[16]{0:T(128)} %lengths_ref.1, bf16[128,1024]{1,0:T(8,128)(2,1)} %query_ref.1, bf16[128,128]{1,0:T(8,128)(2,1)} %key_ref.1, bf16[128,128]{1,0:T(8,128)(2,1)} %value_ref.1, bf16[128,1024]{1,0:T(8,128)(2,1)} %residual_in_ref.1, bf16[1024]{0:T(1024)(128)(2,1)} %gain_ref.1, ...), custom_call_target="tpu_custom_call" | custom-call | tf_op jit(solution)/shard_map/layer/pallas_call | solution.py:607
  103.4 0.0 copy-start
  103.5 1.7 %copy.12 = bf16[128,1024]{1,0:T(8,128)(2,1)} copy(bf16[128,1024]{1,0:T(8,128)(2,1)} %get-tuple-element.8) | data formatting | bytes 524288
  105.2 0.0 copy-done
  105.2 0.8 copy.13
Async XLA Ops:
  103.4 1.7 %copy-start = (bf16[448,512]{1,0:T(8,128)(2,1)S(1)}, bf16[448,512]{1,0:T(8,128)(2,1)}, u32[]{:S(2)}) copy-start(bf16[448,512]{1,0:T(8,128)(2,1)} %get-tuple-element.5) | copy-start | bytes 1376260

commit v10 on v9

--- a/solution.py
+++ b/solution.py
@@ -596,6 +596,11 @@
         return 0
 
     lax.fori_loop(0, 8, sums_sent, 0)
+
+
+def hand_over_kernel(residual_ref, hidden_ref, residual_out, hidden_out):
+    residual_out[...] = residual_ref[...]
+    hidden_out[...] = hidden_ref[...]
 
 
 def on_device(
@@ -642,6 +647,16 @@
         doc_lengths, query_heads, key_heads, value_heads, residual_in,
         norm_gain, gate_weight.T, up_weight.T,
     )
+    residual, hidden = pl.pallas_call(
+        hand_over_kernel,
+        out_shape=(
+            jax.ShapeDtypeStruct((ROWS, KB), jnp.bfloat16),
+            jax.ShapeDtypeStruct((HALF, 4 * ROWS), jnp.bfloat16),
+        ),
+        in_specs=[vmem] * 2,
+        out_specs=(vmem, vmem),
+        name="hand_over",
+    )(residual, hidden)
     return residual, hidden.T
 
 

time: 106 us -> 106 us (level)
  local copies, waits for them, and re-layouts: 2.49 us -> 0 us
  Pallas kernels: 103 us -> 105 us
    unnamed x4 -> x0, local copies, waits for them, and re-layouts: 2.49 us -> none
    pallas_call x0 -> x1, Pallas kernels: none -> 1.97 us  [on_device(): pl.pallas_call(hand_over_kernel, out_shape=(jax.ShapeDtypeStruct((ROWS, K...]
where the time goes in v10:
time: 106 us; the launch traced here: 105 us
  Pallas kernels  105 us (99%)
    pallas_call x1, Pallas kernels, on_device(): pl.pallas_call(layer_kernel, out_shape=(jax.ShapeDtypeStruct((ROWS, KB),...  103 us

profile of v10, /device:TPU:25, one launch (start us, length us, event | category | flops | bytes accessed | tf_op | source)
XLA Modules:
  0.0 105.4 jit_solution(16173168666462471430)
XLA Ops:
  0.6 102.8 %layer.1 = (bf16[128,1024]{1,0:T(8,128)(2,1)}, bf16[448,512]{1,0:T(8,128)(2,1)}) custom-call(s32[16]{0:T(128)} %lengths_ref.1, bf16[128,1024]{1,0:T(8,128)(2,1)} %query_ref.1, bf16[128,128]{1,0:T(8,128)(2,1)} %key_ref.1, bf16[128,128]{1,0:T(8,128)(2,1)} %value_ref.1, bf16[128,1024]{1,0:T(8,128)(2,1)} %residual_in_ref.1, bf16[1024]{0:T(1024)(128)(2,1)} %gain_ref.1, ...), custom_call_target="tpu_custom_call" | custom-call | tf_op jit(solution)/shard_map/layer/pallas_call | solution.py:612
  103.4 2.0 %hand_over.1 = (bf16[128,1024]{1,0:T(8,128)(2,1)}, bf16[448,512]{1,0:T(8,128)(2,1)}) custom-call(bf16[128,1024]{1,0:T(8,128)(2,1)} %get-tuple-element.6.residual_ref, bf16[448,512]{1,0:T(8,128)(2,1)} %get-tuple-element.7.hidden_ref), custom_call_target="tpu_custom_call" | custom-call | tf_op jit(solution)/shard_map/hand_over/pallas_call | solution.py:650
